TPU v7x, 32 devices: a whole 2x2x4 slice. The times are simulated.
32 devices in a mesh: replica: 2 (over y), group: 16 (over z, x, core).
Axes of the slice: x: 2, y: 2, z: 4, core: 2. Of those that a mesh axis runs over, the one named last changes fastest.
Arguments:
- tokens: bfloat16 [4, 4096, 640], P('replica', 'group'), may hold values from -6 to 6
- cotangent: bfloat16 [4, 4096, 640], P('replica', 'group'), may hold values from -6 to 6
- lengths: int32 [4, 2], P('replica'), may hold values from 1 to 3072, 4096 in all within a row
- w_qkv: float32 [640, 1536], P('group'), may hold values from -0.25 to 0.25
- w_out: float32 [1024, 640], P('group'), may hold values from -0.1875 to 0.1875
- w_gu: float32 [640, 4096], P('group'), may hold values from -0.25 to 0.25
- w_down: float32 [2048, 640], P('group'), may hold values from -0.125 to 0.125
- norm_gains: float32 [3072], P('group'), may hold values from 0.5 to 1.5
- first_qkv: float32 [640, 1536], P('group'), may hold values from -80 to 80
- first_out: float32 [1024, 640], P('group'), may hold values from -80 to 80
- first_gu: float32 [640, 4096], P('group'), may hold values from -56 to 56
- first_down: float32 [2048, 640], P('group'), may hold values from -80 to 80
- first_gains: float32 [3072], P('group'), may hold values from -128 to 128
- second_qkv: float32 [640, 1536], P('group'), may hold values from 19.6608 to 81.92
- second_out: float32 [1024, 640], P('group'), may hold values from 16.384 to 65.536
- second_gu: float32 [640, 4096], P('group'), may hold values from 6.5536 to 26.2144
- second_down: float32 [2048, 640], P('group'), may hold values from 16.384 to 65.536
- second_gains: float32 [3072], P('group'), may hold values from 36.0448 to 147.456
Outputs:
- layer_out: bfloat16 [4, 4096, 640], P('replica', 'group')
- token_grad: float32 [4, 4096, 640], P('replica', 'group')
- moment_qkv: float32 [640, 1536], P('group')
- square_qkv: float32 [640, 1536], P('group')
- master_qkv: float32 [640, 1536], P('group')
- moment_out: float32 [1024, 640], P('group')
- square_out: float32 [1024, 640], P('group')
- master_out: float32 [1024, 640], P('group')
- moment_gu: float32 [640, 4096], P('group')
- square_gu: float32 [640, 4096], P('group')
- master_gu: float32 [640, 4096], P('group')
- moment_down: float32 [2048, 640], P('group')
- square_down: float32 [2048, 640], P('group')
- master_down: float32 [2048, 640], P('group')
- moment_gains: float32 [3072], P('group')
- square_gains: float32 [3072], P('group')
- master_gains: float32 [3072], P('group')
Inputs may be any that keep to these rules, and one draw needn't show every extreme that they name: Each row holds two sequences whose lengths sum to 4096.
All inputs are finite; a program needn't handle non-finite values.
Results may differ from a plain program's by a relative error of at most 0.035.
Values may be sent and summed in bfloat16 or wider, within the bound.
No kernel may reach another device: no remote copies, remote signals or barrier semaphores. Data moves between devices by JAX's collectives and lax.ppermute only.
A program may use at most 256 MiB of HBM per device.

v0:
```python
import math

import jax
import jax.numpy as jnp
from jax import lax
from jax.sharding import PartitionSpec as P

D = 640
HQ = 4
HD = 256
FF = 2048
SEG = 256
STEP = 10


EPS_NORM = 1e-06
BETA_ONE = 0.9
BETA_TWO = 0.999
ADAM_EPS = 1e-08
RATE_MATRIX = 0.1
RATE_GAIN = 0.5
DECAY_RATE = 0.1
ROPE_BASE = 1000000.0
NEGATIVE = -1e30
SCALE_SCORE = 0.0625


def rms_norm(values, gain_row):
    factor = lax.rsqrt(jnp.mean(values * values, axis=-1, keepdims=True) + EPS_NORM)
    return values * factor * gain_row


def angles(position, width):
    half_width = width // 2
    frequency = jnp.exp(
        jnp.arange(half_width, dtype=jnp.float32) * (-2.0 * math.log(ROPE_BASE) / width)
    )
    angle_table = position.astype(jnp.float32)[:, None] * frequency[None, :]
    return (jnp.cos(angle_table), jnp.sin(angle_table))


def rotate(values, cosine, sine):
    half_width = values.shape[-1] // 2
    leading = values[..., :half_width]
    trailing = values[..., half_width:]
    return jnp.concatenate(
        [leading * cosine - trailing * sine, trailing * cosine + leading * sine], axis=-1
    )


def layout(lengths, total):
    seq_ends = jnp.cumsum(lengths)
    seq_starts = seq_ends - lengths
    stream_index = jnp.arange(total, dtype=jnp.int32)
    segment = jnp.sum((stream_index[:, None] >= seq_ends[None, :]).astype(jnp.int32), axis=1)
    seq_begin = jnp.max(
        jnp.where(stream_index[:, None] >= seq_starts[None, :], seq_starts[None, :], 0), axis=1
    )
    return (segment, stream_index - seq_begin)


def heads_in(qkv_rows, gain_query, gain_key, cosine, sine):
    row_count = qkv_rows.shape[0]
    queries = qkv_rows[:, : HQ * HD].reshape(row_count, HQ, HD)
    keys_pre = qkv_rows[:, HQ * HD : (HQ + 1) * HD]
    values_pre = qkv_rows[:, (HQ + 1) * HD :]
    query_rot = rotate(rms_norm(queries, gain_query), cosine[:, None, :], sine[:, None, :])
    key_rot = rotate(rms_norm(keys_pre, gain_key), cosine, sine)
    return (query_rot, key_rot, values_pre)


def geglu(gate_up):
    return jax.nn.gelu(gate_up[:, :FF], approximate=True) * gate_up[:, FF:]


def split_gains(gain_all):
    return (
        gain_all[0:D],
        gain_all[D : 2 * D],
        gain_all[2 * D : 3 * D],
        gain_all[3 * D : 4 * D],
        gain_all[4 * D : 4 * D + HD],
        gain_all[4 * D + HD : 4 * D + 2 * HD],
    )


def adam_step(master, moment_one, moment_two, gradient, rate, decay):
    moment_new = BETA_ONE * moment_one + (1.0 - BETA_ONE) * gradient
    square_new = BETA_TWO * moment_two + (1.0 - BETA_TWO) * gradient * gradient
    moment_hat = moment_new / (1.0 - BETA_ONE**STEP)
    square_hat = square_new / (1.0 - BETA_TWO**STEP)
    master_new = master * (1.0 - rate * decay) - rate * moment_hat / (
        jnp.sqrt(square_hat) + ADAM_EPS
    )
    return (moment_new, square_new, master_new)


def per_device(
    tokens,
    cotangent,
    lengths,
    w_qkv,
    w_out,
    w_gu,
    w_down,
    norm_gains,
    first_qkv,
    first_out,
    first_gu,
    first_down,
    first_gains,
    second_qkv,
    second_out,
    second_gu,
    second_down,
    second_gains,
):
    streams = tokens.shape[0]
    row_count = streams * SEG
    members = lax.axis_size("group")
    stream_len = SEG * members
    member_index = lax.axis_index("group")
    tok_rows = tokens.reshape(row_count, D).astype(jnp.float32)
    grad_out = cotangent.reshape(row_count, D).astype(jnp.float32)
    full_qkv, full_out, full_gu, full_down, full_gains = (
        lax.all_gather(w_qkv.astype(jnp.bfloat16), "group", axis=0, tiled=True),
        lax.all_gather(w_out.astype(jnp.bfloat16), "group", axis=0, tiled=True),
        lax.all_gather(w_gu.astype(jnp.bfloat16), "group", axis=0, tiled=True),
        lax.all_gather(w_down.astype(jnp.bfloat16), "group", axis=0, tiled=True),
        lax.all_gather(norm_gains.astype(jnp.bfloat16), "group", axis=0, tiled=True),
    )
    gain_in, gain_pa, gain_pf, gain_po, gain_query, gain_key = split_gains(
        full_gains.astype(jnp.float32)
    )
    segment_all, position_all = jax.vmap(lambda stream_lengths: layout(stream_lengths, stream_len))(
        lengths
    )
    start_row = member_index * SEG
    segment_mine = lax.dynamic_slice_in_dim(segment_all, start_row, SEG, 1)
    position_mine = lax.dynamic_slice_in_dim(position_all, start_row, SEG, 1)
    stream_index = jnp.arange(stream_len, dtype=jnp.int32)
    index_mine = start_row + jnp.arange(SEG, dtype=jnp.int32)
    allowed = (segment_mine[:, :, None] == segment_all[:, None, :]) & (
        index_mine[None, :, None] >= stream_index[None, None, :]
    )
    cosine, sine = angles(position_mine.reshape(row_count), HD)
    normed_in, pull_in = jax.vjp(rms_norm, tok_rows, gain_in)
    input_low = normed_in.astype(jnp.bfloat16)
    qkv_rows = jnp.dot(input_low, full_qkv, preferred_element_type=jnp.float32)

    def project(rows_in, gain_q_in, gain_k_in):
        return heads_in(rows_in, gain_q_in, gain_k_in, cosine, sine)

    head_outs, pull_heads = jax.vjp(project, qkv_rows, gain_query, gain_key)
    query_low = head_outs[0].astype(jnp.bfloat16).reshape(streams, SEG, HQ, HD)
    key_low = head_outs[1].astype(jnp.bfloat16).reshape(streams, SEG, HD)
    value_low = head_outs[2].astype(jnp.bfloat16).reshape(streams, SEG, HD)
    key_all, value_all = (
        lax.all_gather(key_low, "group", axis=1, tiled=True),
        lax.all_gather(value_low, "group", axis=1, tiled=True),
    )

    def scores():
        raw_scores = (
            jnp.einsum("sqhd,skd->shqk", query_low, key_all, preferred_element_type=jnp.float32)
            * SCALE_SCORE
        )
        return jnp.where(allowed[:, None], raw_scores, NEGATIVE)

    score_fwd = scores()
    row_max = jnp.max(score_fwd, axis=-1, keepdims=True)
    exp_fwd = jnp.exp(score_fwd - row_max)
    row_total = jnp.sum(exp_fwd, axis=-1, keepdims=True)
    prob_low = (exp_fwd / row_total).astype(jnp.bfloat16)
    attended = jnp.einsum("shqk,skd->sqhd", prob_low, value_all, preferred_element_type=jnp.float32)
    attn_low = attended.reshape(row_count, HQ * HD).astype(jnp.bfloat16)
    attn_proj = jnp.dot(attn_low, full_out, preferred_element_type=jnp.float32)
    post_attn, pull_attn = jax.vjp(rms_norm, attn_proj, gain_pa)
    middle = tok_rows + post_attn
    normed_ff, pull_ff = jax.vjp(rms_norm, middle, gain_pf)
    ff_low = normed_ff.astype(jnp.bfloat16)
    gate_up = jnp.dot(ff_low, full_gu, preferred_element_type=jnp.float32)
    hidden, pull_geglu = jax.vjp(geglu, gate_up)
    hidden_low = hidden.astype(jnp.bfloat16)
    down_proj = jnp.dot(hidden_low, full_down, preferred_element_type=jnp.float32)
    post_ff, pull_post = jax.vjp(rms_norm, down_proj, gain_po)
    layer_out = (middle + post_ff).astype(jnp.bfloat16).reshape(streams, SEG, D)
    back_qkv, back_out, back_gu, back_down = (
        lax.all_gather(w_qkv.astype(jnp.bfloat16), "group", axis=0, tiled=True),
        lax.all_gather(w_out.astype(jnp.bfloat16), "group", axis=0, tiled=True),
        lax.all_gather(w_gu.astype(jnp.bfloat16), "group", axis=0, tiled=True),
        lax.all_gather(w_down.astype(jnp.bfloat16), "group", axis=0, tiled=True),
    )
    grad_down, grad_gain_po = pull_post(grad_out)
    down_low = grad_down.astype(jnp.bfloat16)
    wgrad_down = jnp.dot(hidden_low.T, down_low, preferred_element_type=jnp.float32)
    grad_hidden = jnp.dot(down_low, back_down.T, preferred_element_type=jnp.float32)
    (grad_gate_up,) = pull_geglu(grad_hidden)
    gate_up_low = grad_gate_up.astype(jnp.bfloat16)
    wgrad_gu = jnp.dot(ff_low.T, gate_up_low, preferred_element_type=jnp.float32)
    grad_normed_ff = jnp.dot(gate_up_low, back_gu.T, preferred_element_type=jnp.float32)
    grad_middle_ff, grad_gain_pf = pull_ff(grad_normed_ff)
    grad_middle = grad_out + grad_middle_ff
    grad_attn_proj, grad_gain_pa = pull_attn(grad_middle)
    proj_low = grad_attn_proj.astype(jnp.bfloat16)
    wgrad_out = jnp.dot(attn_low.T, proj_low, preferred_element_type=jnp.float32)
    grad_attn_low = (
        jnp.dot(proj_low, back_out.T, preferred_element_type=jnp.float32)
        .astype(jnp.bfloat16)
        .reshape(streams, SEG, HQ, HD)
    )
    prob_back = jnp.exp(scores() - row_max) / row_total
    grad_prob = jnp.einsum(
        "sqhd,skd->shqk", grad_attn_low, value_all, preferred_element_type=jnp.float32
    )
    row_dot = jnp.sum(prob_back * grad_prob, axis=-1, keepdims=True)
    score_low = (prob_back * (grad_prob - row_dot)).astype(jnp.bfloat16)
    grad_query = (
        jnp.einsum("shqk,skd->sqhd", score_low, key_all, preferred_element_type=jnp.float32)
        * SCALE_SCORE
    )
    key_terms = (
        jnp.einsum("shqk,sqhd->skd", score_low, query_low, preferred_element_type=jnp.float32)
        * SCALE_SCORE
    )
    value_terms = jnp.einsum(
        "shqk,sqhd->skd", prob_low, grad_attn_low, preferred_element_type=jnp.float32
    )
    grad_key, grad_value = (
        lax.psum_scatter(
            key_terms.astype(jnp.bfloat16), "group", scatter_dimension=1, tiled=True
        ).astype(jnp.float32),
        lax.psum_scatter(
            value_terms.astype(jnp.bfloat16), "group", scatter_dimension=1, tiled=True
        ).astype(jnp.float32),
    )
    grad_qkv, grad_gain_q, grad_gain_k = pull_heads(
        (
            grad_query.reshape(row_count, HQ, HD),
            grad_key.reshape(row_count, HD),
            grad_value.reshape(row_count, HD),
        )
    )
    qkv_low = grad_qkv.astype(jnp.bfloat16)
    wgrad_qkv = jnp.dot(input_low.T, qkv_low, preferred_element_type=jnp.float32)
    grad_normed_in = jnp.dot(qkv_low, back_qkv.T, preferred_element_type=jnp.float32)
    grad_tokens_in, grad_gain_in = pull_in(grad_normed_in)
    token_grad = (grad_middle + grad_tokens_in).reshape(streams, SEG, D)
    wgrad_gains = jnp.concatenate(
        [grad_gain_in, grad_gain_pa, grad_gain_pf, grad_gain_po, grad_gain_q, grad_gain_k]
    )
    shard_qkv, shard_out, shard_gu, shard_down, shard_gains = (
        lax.psum_scatter(
            wgrad_qkv.astype(jnp.bfloat16), "group", scatter_dimension=0, tiled=True
        ).astype(jnp.float32),
        lax.psum_scatter(
            wgrad_out.astype(jnp.bfloat16), "group", scatter_dimension=0, tiled=True
        ).astype(jnp.float32),
        lax.psum_scatter(
            wgrad_gu.astype(jnp.bfloat16), "group", scatter_dimension=0, tiled=True
        ).astype(jnp.float32),
        lax.psum_scatter(
            wgrad_down.astype(jnp.bfloat16), "group", scatter_dimension=0, tiled=True
        ).astype(jnp.float32),
        lax.psum_scatter(
            wgrad_gains.astype(jnp.bfloat16), "group", scatter_dimension=0, tiled=True
        ).astype(jnp.float32),
    )
    shard_qkv, shard_out, shard_gu, shard_down, shard_gains = (
        lax.psum(shard_qkv.astype(jnp.bfloat16), "replica").astype(jnp.float32),
        lax.psum(shard_out.astype(jnp.bfloat16), "replica").astype(jnp.float32),
        lax.psum(shard_gu.astype(jnp.bfloat16), "replica").astype(jnp.float32),
        lax.psum(shard_down.astype(jnp.bfloat16), "replica").astype(jnp.float32),
        lax.psum(shard_gains.astype(jnp.bfloat16), "replica").astype(jnp.float32),
    )
    upd_qkv = adam_step(w_qkv, first_qkv, second_qkv, shard_qkv, RATE_MATRIX, DECAY_RATE)
    upd_out = adam_step(w_out, first_out, second_out, shard_out, RATE_MATRIX, DECAY_RATE)
    upd_gu = adam_step(w_gu, first_gu, second_gu, shard_gu, RATE_MATRIX, DECAY_RATE)
    upd_down = adam_step(w_down, first_down, second_down, shard_down, RATE_MATRIX, DECAY_RATE)
    upd_gains = adam_step(norm_gains, first_gains, second_gains, shard_gains, RATE_GAIN, 0.0)
    return (
        layer_out,
        token_grad,
        upd_qkv[0],
        upd_qkv[1],
        upd_qkv[2],
        upd_out[0],
        upd_out[1],
        upd_out[2],
        upd_gu[0],
        upd_gu[1],
        upd_gu[2],
        upd_down[0],
        upd_down[1],
        upd_down[2],
        upd_gains[0],
        upd_gains[1],
        upd_gains[2],
    )


def solution(mesh):
    in_specs = (
        P("replica", "group", None),
        P("replica", "group", None),
        P("replica", None),
        P("group", None),
        P("group", None),
        P("group", None),
        P("group", None),
        P("group"),
        P("group", None),
        P("group", None),
        P("group", None),
        P("group", None),
        P("group"),
        P("group", None),
        P("group", None),
        P("group", None),
        P("group", None),
        P("group"),
    )
    out_specs = (
        P("replica", "group", None),
        P("replica", "group", None),
        P("group", None),
        P("group", None),
        P("group", None),
        P("group", None),
        P("group", None),
        P("group", None),
        P("group", None),
        P("group", None),
        P("group", None),
        P("group", None),
        P("group", None),
        P("group", None),
        P("group"),
        P("group"),
        P("group"),
    )
    return jax.shard_map(
        per_device, mesh=mesh, in_specs=in_specs, out_specs=out_specs, check_vma=False
    )
```

profile of v0, /device:TPU:0, one launch (start us, length us, event | category | flops | bytes accessed | tf_op | source)
XLA Modules:
  0.0 866.0 jit_solution(3144286851838306413)
XLA Ops:
  7.2 1.6 convert_element_type.149
  11.1 1.3 fusion.55
  13.3 1.3 fusion.113
  15.5 35.8 %all-reduce.9 = bf16[3072]{0:T(1024)(128)(2,1)S(1)} all-reduce(bf16[3072]{0:T(1024)(128)(2,1)S(1)} %dynamic-update-slice), channel_id=1, replica_groups=mesh['replica'=2,'group'=16] {'group'}, use_global_device_ids=true, to_apply=%add.9 | all-reduce | flops 3072 | bytes 12288
  51.4 2.1 fusion.53
  53.6 1.0 all-gather.7.cloned.1.call-done
  54.6 3.1 fusion.115
  58.7 1.8 multiply_cosine_fusion
  62.1 1.8 copy.107
  64.1 1.6 convert_element_type.157
  65.7 1.8 convert_element_type.159
  69.3 4.2 compare_and_fusion
  73.7 2.0 reshape.307
  75.8 2.2 multiply_reduce_fusion.1
  79.4 31.5 %all-gather.11.cloned.1.call-done = bf16[2,4096,256]{2,1,0:T(8,128)(2,1)} async-done(((bf16[2,256,256]{2,1,0:T(8,128)(2,1)}), bf16[2,4096,256]{2,1,0:T(8,128)(2,1)}) %all-gather.11.cloned.1.call-update) | async-done | bytes 4194320 | tf_op jit(solution)/shard_map/all_gather | solution.py:159
  110.9 15.6 %fusion.26 = f32[2,4096,256,4]{2,1,3,0:T(8,128)} fusion(bf16[2,4096,256]{2,1,0:T(8,128)(2,1)} %all-gather.11.cloned.1.call-done, bf16[2,256,4,128]{3,1,0,2:T(8,128)(2,1)S(1)} %bitcast.150, bf16[2,256,4,128]{3,1,0,2:T(8,128)(2,1)S(1)} %bitcast.148), kind=kOutput, calls=%fused_computation.36 | convolution fusion | flops 4297064448 | bytes 38797312 | tf_op jit(solution)/shard_map/sqhd,skd->shqk/dot_general | solution.py:165
  126.5 35.4 %fusion.114 = (f32[2,4,256]{2,1,0:T(4,128)S(1)}, f32[2,4,256,4096]{2,3,1,0:T(8,128)}) fusion(f32[2,4096,256,4]{2,1,3,0:T(8,128)} %fusion.26, pred[2,256,4096]{1,2,0:T(8,128)(4,1)} %compare_and_fusion), kind=kOutput, calls=%fused_computation.190 | output fusion | flops 50335744 | bytes 69214208 | tf_op jit(solution)/shard_map/sub | solution.py:172
  161.9 3.5 all-gather.9.cloned.1.call-done
  165.4 14.3 %fusion.41 = bf16[2,256,4,256]{1,3,2,0:T(8,128)(2,1)S(1)} fusion(bf16[2,4096,256]{1,2,0:T(8,128)(2,1)} %all-gather.9.cloned.1.call-done, f32[2,4,256,4096]{2,3,1,0:T(8,128)} %get-tuple-element.76, f32[2,4,256]{2,1,0:T(4,128)S(1)} %get-tuple-element.75), kind=kOutput, calls=%fused_computation.68 | convolution fusion | flops 4312268800 | bytes 38805504 | tf_op jit(solution)/shard_map/shqk,skd->sqhd/dot_general | solution.py:175
  180.6 1.2 copy.136
  181.8 23.3 %all-gather.13.cloned.1.call-done = bf16[1024,640]{1,0:T(8,128)(2,1)} async-done(((bf16[64,640]{1,0:T(8,128)(2,1)}), bf16[1024,640]{1,0:T(8,128)(2,1)}) %all-gather.13.cloned.1.call-update) | async-done | bytes 1310736 | tf_op jit(solution)/shard_map/all_gather | solution.py:127
  205.1 2.8 multiply_reduce_fusion.8
  208.4 54.3 %all-gather.15.cloned.1.call-done = bf16[640,4096]{1,0:T(8,128)(2,1)} async-done(((bf16[40,4096]{1,0:T(8,128)(2,1)}), bf16[640,4096]{1,0:T(8,128)(2,1)}) %all-gather.15.cloned.1.call-update) | async-done | bytes 5242896 | tf_op jit(solution)/shard_map/all_gather | solution.py:128
  262.7 5.5 fusion.100
  268.2 3.2 copy-done.2
  271.4 2.4 multiply_convert_fusion
  273.8 33.4 %all-gather.17.cloned.1.call-done = bf16[2048,640]{1,0:T(8,128)(2,1)} async-done(((bf16[128,640]{1,0:T(8,128)(2,1)}), bf16[2048,640]{1,0:T(8,128)(2,1)}) %all-gather.17.cloned.1.call-update) | async-done | bytes 2621456 | tf_op jit(solution)/shard_map/all_gather | solution.py:129
  307.2 4.4 multiply_reduce_fusion.6
  311.6 1.1 fusion.50
  312.7 1.4 fusion.47
  314.1 4.9 fusion.40
  319.1 4.1 multiply_reduce_fusion.2
  323.2 1.4 multiply_reduce_fusion.3
  326.5 1.0 convolution_convert_fusion.4
  327.5 1.0 reshape.309
  328.5 23.8 %fusion.1 = (f32[2,4,256]{2,1,0:T(4,128)S(1)}, f32[2,4096,256,4]{2,1,3,0:T(8,128)}) fusion(f32[2,4,256,4096]{2,3,1,0:T(8,128)} %get-tuple-element.76, f32[2,4,256]{2,1,0:T(4,128)S(1)} %get-tuple-element.75, bf16[2,256,4,256]{3,2,1,0:T(4,128)(2,1)S(1)} %reshape.309, bf16[2,4096,256]{1,2,0:T(8,128)(2,1)} %all-gather.9.cloned.1.call-done), kind=kOutput, calls=%fused_computation.3 | convolution fusion | flops 4320131072 | bytes 72368128 | tf_op jit(solution)/shard_map/sqhd,skd->shqk/dot_general | solution.py:213
  352.3 27.8 %fusion.3 = bf16[2,4,256,4096]{2,3,1,0:T(8,128)(2,1)} fusion(f32[2,4096,256,4]{2,1,3,0:T(8,128)} %get-tuple-element.83, f32[2,4,256]{2,1,0:T(4,128)S(1)} %get-tuple-element.82, f32[2,4,256,4096]{2,3,1,0:T(8,128)} %get-tuple-element.76, f32[2,4,256]{2,1,0:T(4,128)S(1)} %get-tuple-element.75), kind=kLoop, calls=%fused_computation.5 | loop fusion | flops 33554432 | bytes 83902464 | tf_op jit(solution)/shard_map/convert_element_type | solution.py:217
  380.1 16.2 %fusion.8 = bf16[2,4096,256]{2,1,0:T(8,128)(2,1)} fusion(bf16[2,4,256,4096]{2,3,1,0:T(8,128)(2,1)} %fusion.3, bf16[2,256,4,128]{3,1,0,2:T(8,128)(2,1)S(1)} %bitcast.151, bf16[2,256,4,128]{3,1,0,2:T(8,128)(2,1)S(1)} %bitcast.149), kind=kOutput, calls=%fused_computation.14 | convolution fusion | flops 4301258752 | bytes 22020096 | tf_op jit(solution)/shard_map/shqk,sqhd->skd/dot_general | solution.py:223
  396.5 16.1 %bitcast_convert_fusion = bf16[2,4096,256]{2,1,0:T(8,128)(2,1)} fusion(bf16[2,256,4,256]{3,2,1,0:T(4,128)(2,1)S(1)} %reshape.309, f32[2,4,256,4096]{2,3,1,0:T(8,128)} %get-tuple-element.76, f32[2,4,256]{2,1,0:T(4,128)S(1)} %get-tuple-element.75), kind=kOutput, calls=%fused_computation.15 | convolution fusion | flops 4313841664 | bytes 38805504 | tf_op jit(solution)/shard_map/shqk,sqhd->skd/dot_general | solution.py:226
  412.6 3.7 convolution_convert_fusion.3
  416.8 4.4 convolution_convert_fusion.1
  421.3 8.8 %convolution_convert_fusion = bf16[640,4096]{1,0:T(8,128)(2,1)} fusion(f32[512,2048]{1,0:T(8,128)} %copy-done.12, f32[512,2048]{1,0:T(8,128)} %copy-done.11, f32[512,640]{1,0:T(8,128)S(1)} %get-tuple-element.50, f32[640]{0:T(1024)S(1)} %get-tuple-element.64, f32[512]{0:T(512)S(1)} %fusion.91), kind=kOutput, calls=%fused_computation.22 | convolution fusion | flops 2692153344 | bytes 14946816 | tf_op jit(solution)/shard_map/dot_general | solution.py:200
  430.2 11.5 %multiply_bitcast_fusion = f32[2,256,4,256]{3,1,2,0:T(8,128)S(1)} fusion(bf16[2,4,256,4096]{2,3,1,0:T(8,128)(2,1)} %fusion.3, bf16[2,4096,256]{2,1,0:T(8,128)(2,1)} %all-gather.11.cloned.1.call-done), kind=kOutput, calls=%fused_computation.52 | convolution fusion | flops 4295491584 | bytes 23068672 | tf_op jit(solution)/shard_map/shqk,skd->sqhd/dot_general | solution.py:219
  443.0 1.3 copy-done.1
  445.9 1.6 copy.133
  447.4 20.2 %reduce-scatter.9.cloned.1.call-done = bf16[2,256,256]{2,1,0:T(8,128)(2,1)} async-done(((bf16[2,4096,256]{2,1,0:T(8,128)(2,1)}), bf16[2,256,256]{2,1,0:T(8,128)(2,1)}) %reduce-scatter.9.cloned.1.call-update) | async-done | bytes 262160 | tf_op jit(solution)/shard_map/reduce_scatter | solution.py:230
  468.6 1.2 fusion.78
  469.8 1.3 multiply_reduce_fusion.9
  471.1 1.2 add_add_fusion.5
  472.4 71.1 %reduce-scatter.7.cloned.1.call-done = bf16[2,256,256]{2,1,0:T(8,128)(2,1)} async-done(((bf16[2,4096,256]{2,1,0:T(8,128)(2,1)}), bf16[2,256,256]{2,1,0:T(8,128)(2,1)}) %reduce-scatter.7.cloned.1.call-update) | async-done | bytes 262160 | tf_op jit(solution)/shard_map/reduce_scatter | solution.py:233
  543.5 4.3 convolution_convert_fusion.2
  548.8 4.1 fusion.54
  554.1 30.8 %all-reduce.10 = bf16[3072]{0:T(1024)(128)(2,1)S(1)} all-reduce(bf16[3072]{0:T(1024)(128)(2,1)S(1)} %dynamic-update-slice.6), channel_id=8, replica_groups=mesh['replica'=2,'group'=16] {'group'}, use_global_device_ids=true, to_apply=%region_34.35.clone | all-reduce | flops 3072 | bytes 12288
  585.0 4.9 psum.39
  590.0 14.8 %reduce-scatter.13.cloned.1.call-done = bf16[64,640]{1,0:T(8,128)(2,1)} async-done(((bf16[1024,640]{1,0:T(8,128)(2,1)}), bf16[64,640]{1,0:T(8,128)(2,1)}) %reduce-scatter.13.cloned.1.call-update) | async-done | bytes 81936 | tf_op jit(solution)/shard_map/reduce_scatter | solution.py:256
  604.8 67.1 %reduce-scatter.17.cloned.1.call-done = bf16[128,640]{1,0:T(8,128)(2,1)} async-done(((bf16[2048,640]{1,0:T(8,128)(2,1)}), bf16[128,640]{1,0:T(8,128)(2,1)}) %reduce-scatter.17.cloned.1.call-update) | async-done | bytes 163856 | tf_op jit(solution)/shard_map/reduce_scatter | solution.py:262
  671.8 81.9 %reduce-scatter.15.cloned.1.call-done = bf16[40,4096]{1,0:T(8,128)(2,1)} async-done(((bf16[640,4096]{1,0:T(8,128)(2,1)}), bf16[40,4096]{1,0:T(8,128)(2,1)}) %reduce-scatter.15.cloned.1.call-update) | async-done | bytes 327696 | tf_op jit(solution)/shard_map/reduce_scatter | solution.py:259
  753.7 64.1 %reduce-scatter.11.cloned.1.call-done = bf16[40,1536]{1,0:T(8,128)(2,1)} async-done(((bf16[640,1536]{1,0:T(8,128)(2,1)}), bf16[40,1536]{1,0:T(8,128)(2,1)}) %reduce-scatter.11.cloned.1.call-update) | async-done | bytes 122896 | tf_op jit(solution)/shard_map/reduce_scatter | solution.py:253
  818.5 1.4 fusion.49
  819.9 32.5 %all-reduce.14.cloned.1.call-done = (bf16[40,1536]{1,0:T(8,128)(2,1)}, bf16[64,640]{1,0:T(8,128)(2,1)}, bf16[40,4096]{1,0:T(8,128)(2,1)}, bf16[128,640]{1,0:T(8,128)(2,1)}) async-done(((bf16[40,1536]{1,0:T(8,128)(2,1)}, bf16[64,640]{1,0:T(8,128)(2,1)}, bf16[40,4096]{1,0:T(8,128)(2,1)}, bf16[128,640]{1,0:T(8,128)(2,1)}), (bf16[40,1536]{1,0:T(8,128)(2,1)}, bf16[64,640]{1,0:T(8,128)(2,1)}, ...) | async-done | bytes 696336 | tf_op jit(solution)/shard_map/psum | solution.py:270
  852.4 2.0 divide_subtract_fusion.3
  854.4 2.2 divide_subtract_fusion.2
  856.6 1.1 divide_subtract_fusion.1
  857.7 1.5 divide_subtract_fusion
  (216 shorter events, 19.3 us)
Async XLA Ops:
  7.2 47.4 %all-gather.7.cloned.1.call-start = ((), (), s32[]{:S(2)}) async-start(), calls=%async_computation.6 | async-start | bytes 2088960 | tf_op jit(solution)/shard_map/all_gather | solution.py:126
  8.9 102.1 %all-gather.11.cloned.1.call-start = ((), (), s32[]{:S(2)}) async-start(), calls=%async_computation.8 | async-start | bytes 4456448 | tf_op jit(solution)/shard_map/all_gather | solution.py:159
  13.0 40.5 %copy-start.44 = (f32[512]{0:T(512)}, f32[512]{0:T(512)S(1)}, u32[]{:S(2)}) copy-start(f32[512]{0:T(512)S(1)} %rsqrt.60) | copy-start | bytes 6148
  13.3 45.4 %copy-start.46 = (f32[1,2,2,128]{3,1,2,0:T(2,128)}, f32[1,2,2,128]{3,1,2,0:T(2,128)S(1)}, u32[]{:S(2)}) copy-start(f32[1,2,2,128]{3,1,2,0:T(2,128)S(1)} %copy.135) | copy-start | bytes 6148
  51.4 7.3 copy-start.58
  51.4 6.6 copy-start.52
  51.4 26.8 %copy-start.54 = (f32[256]{0:T(256)}, f32[256]{0:T(256)S(1)}, u32[]{:S(2)}) copy-start(f32[256]{0:T(256)S(1)} %get-tuple-element.67) | copy-start | bytes 3076
  51.4 6.3 copy-start.40
  57.8 4.4 copy-start.8
  58.0 6.0 copy-start.42
  60.5 18.2 %copy-start.14 = (f32[512,128]{1,0:T(8,128)}, f32[512,128]{1,0:T(8,128)S(1)}, u32[]{:S(2)}) copy-start(f32[512,128]{1,0:T(8,128)S(1)} %get-tuple-element.69) | copy-start | bytes 786436
  61.4 104.1 %all-gather.9.cloned.1.call-start = ((), (), s32[]{:S(2)}) async-start(), calls=%async_computation.7 | async-start | bytes 4456448 | tf_op jit(solution)/shard_map/all_gather | solution.py:160
  62.1 5.5 copy-start.23
  64.0 141.1 %all-gather.13.cloned.1.call-start = ((), (), s32[]{:S(2)}) async-start(), calls=%async_computation.9 | async-start | bytes 1392640 | tf_op jit(solution)/shard_map/all_gather | solution.py:127
  65.7 197.0 %all-gather.15.cloned.1.call-start = ((), (), s32[]{:S(2)}) async-start(), calls=%async_computation.10 | async-start | bytes 5570560 | tf_op jit(solution)/shard_map/all_gather | solution.py:128
  67.6 239.6 %all-gather.17.cloned.1.call-start = ((), (), s32[]{:S(2)}) async-start(), calls=%async_computation.11 | async-start | bytes 2785280 | tf_op jit(solution)/shard_map/all_gather | solution.py:129
  68.3 399.3 %reduce-scatter.9.cloned.1.call-start = ((), (), s32[]{:S(2)}) async-start(), calls=%async_computation.13 | async-start | bytes 4456448 | tf_op jit(solution)/shard_map/reduce_scatter | solution.py:230
  68.6 5.0 copy-start.9
  73.7 4.4 copy-start
  79.4 47.1 %copy-start.18 = (bf16[512,4,128]{2,0,1:T(8,128)(2,1)}, bf16[512,4,128]{2,0,1:T(8,128)(2,1)S(1)}, u32[]{:S(2)}) copy-start(bf16[512,4,128]{2,0,1:T(8,128)(2,1)S(1)} %get-tuple-element.55) | copy-start | bytes 1572868
  79.4 47.1 %copy-start.20 = (bf16[512,4,128]{2,0,1:T(8,128)(2,1)}, bf16[512,4,128]{2,0,1:T(8,128)(2,1)S(1)}, u32[]{:S(2)}) copy-start(bf16[512,4,128]{2,0,1:T(8,128)(2,1)S(1)} %get-tuple-element.56) | copy-start | bytes 1572868
  273.8 37.8 %copy-start.10 = (bf16[2,256,640]{2,1,0:T(8,128)(2,1)S(1)}, bf16[2,256,640]{2,1,0:T(8,128)(2,1)}, u32[]{:S(2)}) copy-start(bf16[2,256,640]{2,1,0:T(8,128)(2,1)} %param.19) | copy-start | bytes 1966084
  307.2 6.9 copy-start.3
  312.7 6.4 slice-start
  314.1 5.0 copy-start.26
  314.1 5.0 slice-start.1
  319.1 4.1 copy-start.11
  319.1 4.1 copy-start.12
  352.3 27.8 %copy-start.19 = (bf16[512,4,128]{2,0,1:T(8,128)(2,1)S(1)}, bf16[512,4,128]{2,0,1:T(8,128)(2,1)}, u32[]{:S(2)}) copy-start(bf16[512,4,128]{2,0,1:T(8,128)(2,1)} %copy-done.18) | copy-start | bytes 1572868
  352.3 27.8 %copy-start.21 = (bf16[512,4,128]{2,0,1:T(8,128)(2,1)S(1)}, bf16[512,4,128]{2,0,1:T(8,128)(2,1)}, u32[]{:S(2)}) copy-start(bf16[512,4,128]{2,0,1:T(8,128)(2,1)} %copy-done.20) | copy-start | bytes 1572868
  396.4 147.1 %reduce-scatter.7.cloned.1.call-start = ((), (), s32[]{:S(2)}) async-start(), calls=%async_computation.12 | async-start | bytes 4456448 | tf_op jit(solution)/shard_map/reduce_scatter | solution.py:233
  412.6 4.2 copy-start.22
  412.6 192.2 %reduce-scatter.13.cloned.1.call-start = ((), (), s32[]{:S(2)}) async-start(), calls=%async_computation.15 | async-start | bytes 1392640 | tf_op jit(solution)/shard_map/reduce_scatter | solution.py:256
  416.4 255.5 %reduce-scatter.17.cloned.1.call-start = ((), (), s32[]{:S(2)}) async-start(), calls=%async_computation.17 | async-start | bytes 2785280 | tf_op jit(solution)/shard_map/reduce_scatter | solution.py:262
  421.3 332.4 %reduce-scatter.15.cloned.1.call-start = ((), (), s32[]{:S(2)}) async-start(), calls=%async_computation.16 | async-start | bytes 5570560 | tf_op jit(solution)/shard_map/reduce_scatter | solution.py:259
  430.2 387.6 %reduce-scatter.11.cloned.1.call-start = ((), (), s32[]{:S(2)}) async-start(), calls=%async_computation.14 | async-start | bytes 2088960 | tf_op jit(solution)/shard_map/reduce_scatter | solution.py:253
  445.8 22.8 %copy-start.47 = (f32[1,2,2,128]{3,1,2,0:T(2,128)S(1)}, f32[1,2,2,128]{3,1,2,0:T(2,128)}, u32[]{:S(2)}) copy-start(f32[1,2,2,128]{3,1,2,0:T(2,128)} %copy-done.46) | copy-start | bytes 6148
  445.8 22.8 %copy-start.59 = (f32[128]{0:T(128)S(1)}, f32[128]{0:T(128)}, u32[]{:S(2)}) copy-start(f32[128]{0:T(128)} %copy-done.58) | copy-start | bytes 1540
  445.8 24.0 %copy-start.43 = (f32[512]{0:T(512)S(1)}, f32[512]{0:T(512)}, u32[]{:S(2)}) copy-start(f32[512]{0:T(512)} %copy-done.42) | copy-start | bytes 6148
  445.8 24.0 %copy-start.53 = (f32[256]{0:T(256)S(1)}, f32[256]{0:T(256)}, u32[]{:S(2)}) copy-start(f32[256]{0:T(256)} %copy-done.52) | copy-start | bytes 3076
  447.4 23.7 %copy-start.49 = (f32[512]{0:T(512)S(1)}, f32[512]{0:T(512)}, u32[]{:S(2)}) copy-start(f32[512]{0:T(512)} %copy-done.48) | copy-start | bytes 6148
  447.4 96.0 %copy-start.27 = (bf16[512,640]{1,0:T(8,128)(2,1)S(1)}, bf16[512,640]{1,0:T(8,128)(2,1)}, u32[]{:S(2)}) copy-start(bf16[512,640]{1,0:T(8,128)(2,1)} %fusion.53) | copy-start | bytes 1966084
  472.4 75.4 %copy-start.31 = (f32[512,256]{1,0:T(8,128)}, f32[512,256]{1,0:T(8,128)S(1)}, u32[]{:S(2)}) copy-start(f32[512,256]{1,0:T(8,128)S(1)} %add_add_fusion.5) | copy-start | bytes 1572868
  543.5 5.2 copy-start.7
  543.5 5.2 copy-start.41
  543.5 5.2 copy-start.45
  547.8 304.6 %all-reduce.14.cloned.1.call-start = ((), (), s32[]{:S(2)}) async-start(), calls=%async_computation.18 | async-start | bytes 1392640 | tf_op jit(solution)/shard_map/psum | solution.py:270
  548.7 4.4 copy-start.57
  548.7 4.6 copy-start.60
  548.7 4.8 copy-start.56
  548.7 269.1 %copy-start.51 = (f32[1,2,2,128]{3,1,2,0:T(2,128)S(1)}, f32[1,2,2,128]{3,1,2,0:T(2,128)}, u32[]{:S(2)}) copy-start(f32[1,2,2,128]{3,1,2,0:T(2,128)} %copy-done.50) | copy-start | bytes 6148
  548.7 269.1 %copy-start.61 = (f32[192]{0:T(256)S(1)}, f32[192]{0:T(256)}, u32[]{:S(2)}) copy-start(f32[192]{0:T(256)} %param.25) | copy-start | bytes 2308
  548.7 269.1 %copy-start.62 = (f32[192]{0:T(256)S(1)}, f32[192]{0:T(256)}, u32[]{:S(2)}) copy-start(f32[192]{0:T(256)} %param.35) | copy-start | bytes 2308
  548.8 269.1 %copy-start.63 = (f32[192]{0:T(256)S(1)}, f32[192]{0:T(256)}, u32[]{:S(2)}) copy-start(f32[192]{0:T(256)} %param.30) | copy-start | bytes 2308
  548.8 269.7 %copy-start.5 = (f32[512,640]{1,0:T(8,128)S(1)}, f32[512,640]{1,0:T(8,128)}, u32[]{:S(2)}) copy-start(f32[512,640]{1,0:T(8,128)} %copy-done.4) | copy-start | bytes 3932164
  818.5 35.9 %copy-start.25 = (f32[40,1536]{1,0:T(8,128)S(1)}, f32[40,1536]{1,0:T(8,128)}, u32[]{:S(2)}) copy-start(f32[40,1536]{1,0:T(8,128)} %param.21) | copy-start | bytes 737284
  819.9 36.8 %copy-start.24 = (f32[128,640]{1,0:T(8,128)S(1)}, f32[128,640]{1,0:T(8,128)}, u32[]{:S(2)}) copy-start(f32[128,640]{1,0:T(8,128)} %param.24) | copy-start | bytes 983044
  819.9 36.8 %copy-start.33 = (f32[128,640]{1,0:T(8,128)S(1)}, f32[128,640]{1,0:T(8,128)}, u32[]{:S(2)}) copy-start(f32[128,640]{1,0:T(8,128)} %param.34) | copy-start | bytes 983044
  819.9 36.8 %copy-start.34 = (f32[128,640]{1,0:T(8,128)S(1)}, f32[128,640]{1,0:T(8,128)}, u32[]{:S(2)}) copy-start(f32[128,640]{1,0:T(8,128)} %param.29) | copy-start | bytes 983044
  852.4 4.3 copy-start.35
  854.4 3.4 copy-start.13
  854.4 3.4 copy-start.29
  854.4 3.4 copy-start.30
  854.4 3.4 copy-start.32
  (17 other events, 23.3 us)
Sparse Core Ops, SparseCore 0:
  10.9 43.6 all-gather.6
  61.5 49.4 all-gather.10
  113.7 51.6 all-gather.8
  168.1 36.9 all-gather.12
  207.8 54.7 all-gather.14
  265.4 41.7 all-gather.16
  396.5 71.0 reduce-scatter.8
  472.0 71.4 reduce-scatter.6
  547.1 57.5 reduce-scatter.12
  608.8 62.9 reduce-scatter.16
  676.2 77.4 reduce-scatter.14
  757.7 60.0 reduce-scatter.10
  820.4 31.8 all-reduce.13
where the time goes:
time: 871 us; the launch traced here: 866 us
  waiting for transfers between devices  499 us (57%)
  matrix products  149 us (17%)
  other arithmetic  108 us (12%)
  blocking collectives  71.5 us (8%)
  local copies, waits for them, and re-layouts  21.7 us (2%)
  between operations  16.3 us (2%)
    reduce_scatter x1, waiting for transfers between devices, per_device(): lax.psum_scatter(wgrad_gu.astype(jnp.bfloat16), 'group', scatter_dimensio...  81.9 us
    reduce_scatter x1, waiting for transfers between devices, per_device(): lax.psum_scatter(value_terms.astype(jnp.bfloat16), 'group', scatter_dimen...  71.1 us
    reduce_scatter x1, waiting for transfers between devices, per_device(): lax.psum_scatter(wgrad_down.astype(jnp.bfloat16), 'group', scatter_dimens...  67.1 us
    unnamed x2, blocking collectives  66.6 us
    reduce_scatter x1, waiting for transfers between devices, per_device(): lax.psum_scatter(wgrad_qkv.astype(jnp.bfloat16), 'group', scatter_dimensi...  64.1 us
    all_gather x1, waiting for transfers between devices, per_device(): lax.all_gather(w_gu.astype(jnp.bfloat16), 'group', axis=0, tiled=True)  54.3 us
    sub x1, other arithmetic, per_device(): exp_fwd = jnp.exp(score_fwd - row_max)  35.4 us
    all_gather x1, waiting for transfers between devices, per_device(): lax.all_gather(w_down.astype(jnp.bfloat16), 'group', axis=0, tiled=True)  33.4 us
  transfers between devices with their start and end apart: 13, of which 13 were waited for; matrix products, arithmetic and copies ran while one was open for 19% of the time, Pallas kernels for 0%

commit v1 on v0

v1 whole, which is shorter than its diff:
```python
import math

import jax
import jax.numpy as jnp
from jax import lax
from jax.experimental import pallas as pl
from jax.experimental.pallas import tpu as pltpu
from jax.sharding import PartitionSpec as P

D = 640
HQ = 4
HD = 256
FF = 2048
SEG = 256
STEP = 10


EPS_NORM = 1e-06
BETA_ONE = 0.9
BETA_TWO = 0.999
ADAM_EPS = 1e-08
RATE_MATRIX = 0.1
RATE_GAIN = 0.5
DECAY_RATE = 0.1
ROPE_BASE = 1000000.0
NEGATIVE = -1e30
SCALE_SCORE = 0.0625


def rms_norm(values, gain_row):
    factor = lax.rsqrt(jnp.mean(values * values, axis=-1, keepdims=True) + EPS_NORM)
    return values * factor * gain_row


def angles(position, width):
    half_width = width // 2
    frequency = jnp.exp(
        jnp.arange(half_width, dtype=jnp.float32) * (-2.0 * math.log(ROPE_BASE) / width)
    )
    angle_table = position.astype(jnp.float32)[:, None] * frequency[None, :]
    return (jnp.cos(angle_table), jnp.sin(angle_table))


def rotate(values, cosine, sine):
    half_width = values.shape[-1] // 2
    leading = values[..., :half_width]
    trailing = values[..., half_width:]
    return jnp.concatenate(
        [leading * cosine - trailing * sine, trailing * cosine + leading * sine], axis=-1
    )


def layout(lengths, total):
    seq_ends = jnp.cumsum(lengths)
    seq_starts = seq_ends - lengths
    stream_index = jnp.arange(total, dtype=jnp.int32)
    segment = jnp.sum((stream_index[:, None] >= seq_ends[None, :]).astype(jnp.int32), axis=1)
    seq_begin = jnp.max(
        jnp.where(stream_index[:, None] >= seq_starts[None, :], seq_starts[None, :], 0), axis=1
    )
    return (segment, stream_index - seq_begin)


def heads_in(qkv_rows, gain_query, gain_key, cosine, sine):
    row_count = qkv_rows.shape[0]
    queries = qkv_rows[:, : HQ * HD].reshape(row_count, HQ, HD)
    keys_pre = qkv_rows[:, HQ * HD : (HQ + 1) * HD]
    values_pre = qkv_rows[:, (HQ + 1) * HD :]
    query_rot = rotate(rms_norm(queries, gain_query), cosine[:, None, :], sine[:, None, :])
    key_rot = rotate(rms_norm(keys_pre, gain_key), cosine, sine)
    return (query_rot, key_rot, values_pre)


def geglu(gate_up):
    return jax.nn.gelu(gate_up[:, :FF], approximate=True) * gate_up[:, FF:]


def split_gains(gain_all):
    return (
        gain_all[0:D],
        gain_all[D : 2 * D],
        gain_all[2 * D : 3 * D],
        gain_all[3 * D : 4 * D],
        gain_all[4 * D : 4 * D + HD],
        gain_all[4 * D + HD : 4 * D + 2 * HD],
    )


def adam_step(master, moment_one, moment_two, gradient, rate, decay):
    moment_new = BETA_ONE * moment_one + (1.0 - BETA_ONE) * gradient
    square_new = BETA_TWO * moment_two + (1.0 - BETA_TWO) * gradient * gradient
    moment_hat = moment_new / (1.0 - BETA_ONE**STEP)
    square_hat = square_new / (1.0 - BETA_TWO**STEP)
    master_new = master * (1.0 - rate * decay) - rate * moment_hat / (
        jnp.sqrt(square_hat) + ADAM_EPS
    )
    return (moment_new, square_new, master_new)


LOG2E = 1.4426950408889634
KEYS = 512
MEMBERS = 16
NT = (((1,), (1,)), ((), ()))
TN = (((0,), (0,)), ((), ()))
F32 = jnp.float32
BF16 = jnp.bfloat16


def step_z(values):
    return lax.ppermute(values, "group", [(i, (i + 4) % MEMBERS) for i in range(MEMBERS)])


def swap_x(values):
    return lax.ppermute(values, "group", [(i, i ^ 2) for i in range(MEMBERS)])


def swap_core(values):
    return lax.ppermute(values, "group", [(i, i ^ 1) for i in range(MEMBERS)])


def gather_blocks(own):
    lines = [own]
    for _ in range(3):
        lines.append(step_z(lines[-1]))
    near = []
    for line in lines:
        near += [line, swap_x(line)]
    return near + [swap_core(block) for block in near]


def scatter_blocks(far, near_far, near):
    running = None
    for k in (3, 2, 1, 0):
        came = swap_core(far[k]).astype(F32)
        over = swap_x((near_far[k].astype(F32) + came[1]).astype(BF16))
        total = near[k].astype(F32) + came[0] + over.astype(F32)
        if running is not None:
            total = total + running.astype(F32)
        if k:
            running = step_z(total.astype(BF16))
    return total


def key_range(info, stream):
    first = info[0]
    bound = info[4 + stream]
    last = first + SEG - 1
    low = jnp.where(first >= bound, bound, 0)
    high = jnp.where(last >= bound, bound, 0)
    begin = low // KEYS
    diagonal = first // KEYS
    clear = jnp.clip((high + KEYS - 1) // KEYS, begin, diagonal)
    return first, bound, begin, clear, diagonal


def load_blocks(info, blocks, kv, sem):
    z, x, c = info[1], info[2], info[3]
    copies = []
    for place in range(MEMBERS):
        cr, k, xr = place // 8, place // 2 % 4, place % 2
        owner = ((z - k) & 3) * 4 + (x ^ xr) * 2 + (c ^ cr)
        copies.append(pltpu.make_async_copy(blocks[place], kv.at[owner], sem.at[place]))
    for copy in copies:
        copy.start()
    return copies


def forward_kernel(info, q_ref, *refs):
    blocks = refs[:MEMBERS]
    o_ref, lse_ref, kv, acc, total, sem = refs[MEMBERS:]
    copies = load_blocks(info, blocks, kv, sem)
    for copy in copies:
        copy.wait()
    for stream in range(2):
        first, bound, begin, clear, diagonal = key_range(info, stream)
        acc[...] = jnp.zeros_like(acc)
        total[...] = jnp.zeros_like(total)

        def visit(j, masked):
            keys = kv[pl.ds(2 * j, 2), stream, :, 0:HD].reshape(KEYS, HD)
            values = kv[pl.ds(2 * j, 2), stream, :, HD : 2 * HD].reshape(KEYS, HD)
            if masked:
                row = first + lax.broadcasted_iota(jnp.int32, (SEG, KEYS), 0)
                col = j * KEYS + lax.broadcasted_iota(jnp.int32, (SEG, KEYS), 1)
                mask = (col <= row) & (col >= jnp.where(row >= bound, bound, 0))
            for head in range(HQ):
                rows = slice(head * SEG, (head + 1) * SEG)
                query = q_ref[stream * SEG : (stream + 1) * SEG, head * HD : (head + 1) * HD]
                score = lax.dot_general(query, keys, NT, preferred_element_type=F32)
                prob = jnp.exp2(score * (SCALE_SCORE * LOG2E))
                if masked:
                    prob = jnp.where(mask, prob, 0.0)
                total[rows] += (
                    prob[:, 0:128] + prob[:, 128:256] + prob[:, 256:384] + prob[:, 384:512]
                )
                acc[rows] += jnp.dot(prob.astype(BF16), values, preferred_element_type=F32)

        def masked_step(j, carry):
            visit(j, True)
            return carry

        def clear_step(j, carry):
            visit(j, False)
            return carry

        lax.fori_loop(begin, clear, masked_step, 0)
        lax.fori_loop(clear, diagonal, clear_step, 0)
        masked_step(diagonal, 0)
        for head in range(HQ):
            rows = slice(head * SEG, (head + 1) * SEG)
            part = total[rows]
            out = acc[rows] / jnp.sum(part, axis=1, keepdims=True)
            o_ref[stream * SEG : (stream + 1) * SEG, head * HD : (head + 1) * HD] = out.astype(BF16)
            lse_ref[stream, :, rows] = jnp.log2(jnp.sum(part.T, axis=0, keepdims=True))


def attention_forward(info, query, blocks):
    return pl.pallas_call(
        forward_kernel,
        out_shape=(
            jax.ShapeDtypeStruct((2 * SEG, HQ * HD), BF16),
            jax.ShapeDtypeStruct((2, 1, HQ * SEG), F32),
        ),
        in_specs=[
            pl.BlockSpec(memory_space=pltpu.SMEM),
            pl.BlockSpec(memory_space=pltpu.VMEM),
        ]
        + [pl.BlockSpec(memory_space=pl.ANY)] * MEMBERS,
        out_specs=(
            pl.BlockSpec(memory_space=pltpu.VMEM),
            pl.BlockSpec(memory_space=pltpu.VMEM),
        ),
        scratch_shapes=[
            pltpu.VMEM((MEMBERS, 2, SEG, 2 * HD), BF16),
            pltpu.VMEM((HQ * SEG, HD), F32),
            pltpu.VMEM((HQ * SEG, 128), F32),
            pltpu.SemaphoreType.DMA((MEMBERS,)),
        ],
        compiler_params=pltpu.CompilerParams(vmem_limit_bytes=40 * 1024 * 1024),
        cost_estimate=pl.CostEstimate(
            flops=7_000_000_000, bytes_accessed=11_000_000, transcendentals=7_000_000
        ),
        name="attention_forward",
    )(info, query, *blocks)


def backward_kernel(info, q_ref, o_ref, do_ref, lse_ref, *refs):
    blocks = refs[:MEMBERS]
    dq_ref = refs[MEMBERS]
    far = refs[MEMBERS + 1 : MEMBERS + 5]
    near_far = refs[MEMBERS + 5 : MEMBERS + 9]
    near = refs[MEMBERS + 9 : MEMBERS + 13]
    kv, dkv, qs, qt, dos, dot_, dqt, sem, out_sem = refs[MEMBERS + 13 :]
    copies = load_blocks(info, blocks, kv, sem)
    z, x, c = info[1], info[2], info[3]

    def clean(place, carry):
        dkv[place] = jnp.zeros((2, SEG, 2 * HD), BF16)
        return carry

    lax.fori_loop(0, MEMBERS, clean, 0)
    for copy in copies:
        copy.wait()
    for stream in range(2):
        first, bound, begin, clear, diagonal = key_range(info, stream)
        parts = []
        for head in range(HQ):
            rows = slice(head * SEG, (head + 1) * SEG)
            at = (slice(stream * SEG, (stream + 1) * SEG), slice(head * HD, (head + 1) * HD))
            query = q_ref[at]
            grad = do_ref[at]
            qs[rows] = query
            dos[rows] = grad
            qt[:, rows] = query.T
            dot_[:, rows] = grad.T
            both = grad.astype(F32) * o_ref[at].astype(F32)
            parts.append(
                jnp.sum((both[:, 0:128] + both[:, 128:256]).T, axis=0, keepdims=True)
            )
        delta = jnp.concatenate(parts, axis=1)
        lse = lse_ref[stream]
        dqt[...] = jnp.zeros_like(dqt)

        def visit(j, masked):
            keys = kv[pl.ds(2 * j, 2), stream, :, 0:HD].reshape(KEYS, HD)
            values = kv[pl.ds(2 * j, 2), stream, :, HD : 2 * HD].reshape(KEYS, HD)
            score = jnp.dot(keys, qt[...], preferred_element_type=F32)
            prob = jnp.exp2(score * (SCALE_SCORE * LOG2E) - lse)
            if masked:
                shape = (KEYS, HQ * SEG)
                row = first + (lax.broadcasted_iota(jnp.int32, shape, 1) & (SEG - 1))
                col = j * KEYS + lax.broadcasted_iota(jnp.int32, shape, 0)
                mask = (col <= row) & (col >= jnp.where(row >= bound, bound, 0))
                prob = jnp.where(mask, prob, 0.0)
            dprob = jnp.dot(values, dot_[...], preferred_element_type=F32)
            dscore = (prob * (dprob - delta)).astype(BF16)
            dv = jnp.dot(prob.astype(BF16), dos[...], preferred_element_type=F32).astype(BF16)
            dk = jnp.dot(dscore, qs[...], preferred_element_type=F32)
            dk = (dk * SCALE_SCORE).astype(BF16)
            dqt[...] += jnp.dot(keys.T, dscore, preferred_element_type=F32)
            for core in range(2):
                place = (core ^ c) * 8 + (((j >> 1) - z) & 3) * 2 + ((j & 1) ^ x)
                dkv[place, stream, :, 0:HD] = dk[core * SEG : (core + 1) * SEG]
                dkv[place, stream, :, HD : 2 * HD] = dv[core * SEG : (core + 1) * SEG]

        def masked_step(j, carry):
            visit(j, True)
            return carry

        def clear_step(j, carry):
            visit(j, False)
            return carry

        lax.fori_loop(begin, clear, masked_step, 0)
        lax.fori_loop(clear, diagonal, clear_step, 0)
        masked_step(diagonal, 0)
        for head in range(HQ):
            rows = slice(head * SEG, (head + 1) * SEG)
            at = (slice(stream * SEG, (stream + 1) * SEG), slice(head * HD, (head + 1) * HD))
            dq_ref[at] = dqt[:, rows].T * SCALE_SCORE
    outs = []
    for k in range(4):
        outs.append((dkv.at[pl.ds(8 + 2 * k, 2)], far[k]))
        outs.append((dkv.at[2 * k + 1], near_far[k]))
        outs.append((dkv.at[2 * k], near[k]))
    copies = [
        pltpu.make_async_copy(source, target, out_sem.at[n])
        for n, (source, target) in enumerate(outs)
    ]
    for copy in copies:
        copy.start()
    for copy in copies:
        copy.wait()


def attention_backward(info, query, out, grad_out, lse, blocks):
    one = jax.ShapeDtypeStruct((2, SEG, 2 * HD), BF16)
    two = jax.ShapeDtypeStruct((2, 2, SEG, 2 * HD), BF16)
    vmem = pl.BlockSpec(memory_space=pltpu.VMEM)
    anywhere = pl.BlockSpec(memory_space=pl.ANY)
    result = pl.pallas_call(
        backward_kernel,
        out_shape=[jax.ShapeDtypeStruct((2 * SEG, HQ * HD), F32)] + [two] * 4 + [one] * 8,
        in_specs=[pl.BlockSpec(memory_space=pltpu.SMEM)] + [vmem] * 4 + [anywhere] * MEMBERS,
        out_specs=[vmem] + [anywhere] * 12,
        scratch_shapes=[
            pltpu.VMEM((MEMBERS, 2, SEG, 2 * HD), BF16),
            pltpu.VMEM((MEMBERS, 2, SEG, 2 * HD), BF16),
            pltpu.VMEM((HQ * SEG, HD), BF16),
            pltpu.VMEM((HD, HQ * SEG), BF16),
            pltpu.VMEM((HQ * SEG, HD), BF16),
            pltpu.VMEM((HD, HQ * SEG), BF16),
            pltpu.VMEM((HD, HQ * SEG), F32),
            pltpu.SemaphoreType.DMA((MEMBERS,)),
            pltpu.SemaphoreType.DMA((12,)),
        ],
        compiler_params=pltpu.CompilerParams(vmem_limit_bytes=52 * 1024 * 1024),
        cost_estimate=pl.CostEstimate(
            flops=17_000_000_000, bytes_accessed=24_000_000, transcendentals=7_000_000
        ),
        name="attention_backward",
    )(info, query, out, grad_out, lse, *blocks)
    return result[0], result[1:5], result[5:9], result[9:13]


def per_device(
    tokens,
    cotangent,
    lengths,
    w_qkv,
    w_out,
    w_gu,
    w_down,
    norm_gains,
    first_qkv,
    first_out,
    first_gu,
    first_down,
    first_gains,
    second_qkv,
    second_out,
    second_gu,
    second_down,
    second_gains,
):
    streams = tokens.shape[0]
    row_count = streams * SEG
    member_index = lax.axis_index("group")
    tok_rows = tokens.reshape(row_count, D).astype(F32)
    grad_out = cotangent.reshape(row_count, D).astype(F32)
    qkv_rows_low = w_qkv.astype(BF16)
    gain_count = norm_gains.shape[0]
    gain_row = jnp.pad(norm_gains.astype(BF16), (0, qkv_rows_low.shape[1] - gain_count))
    first_rows = lax.all_gather(
        jnp.concatenate([qkv_rows_low, gain_row[None]], axis=0), "group", axis=0, tiled=False
    )
    full_qkv = first_rows[:, :-1].reshape(D, -1)
    full_gains = first_rows[:, -1, :gain_count].reshape(-1)
    out_rows = w_out.shape[0]
    mixed = lax.all_gather(
        jnp.concatenate([w_out.astype(BF16), w_down.astype(BF16)], axis=0),
        "group",
        axis=0,
        tiled=False,
    )
    full_out = mixed[:, :out_rows].reshape(HQ * HD, D)
    full_down = mixed[:, out_rows:].reshape(FF, D)
    full_gu = lax.all_gather(w_gu.astype(BF16), "group", axis=0, tiled=True)
    gain_in, gain_pa, gain_pf, gain_po, gain_query, gain_key = split_gains(full_gains.astype(F32))
    start_row = member_index * SEG
    index_mine = start_row + jnp.arange(SEG, dtype=jnp.int32)
    boundary = lengths[:, 0]
    position_mine = index_mine[None, :] - jnp.where(
        index_mine[None, :] >= boundary[:, None], boundary[:, None], 0
    )
    info = jnp.concatenate(
        [
            jnp.stack([start_row, member_index // 4, member_index // 2 % 2, member_index % 2]),
            boundary,
        ]
    ).astype(jnp.int32)
    cosine, sine = angles(position_mine.reshape(row_count), HD)
    normed_in, pull_in = jax.vjp(rms_norm, tok_rows, gain_in)
    input_low = normed_in.astype(BF16)
    qkv_rows = jnp.dot(input_low, full_qkv, preferred_element_type=F32)

    def project(rows_in, gain_q_in, gain_k_in):
        return heads_in(rows_in, gain_q_in, gain_k_in, cosine, sine)

    head_outs, pull_heads = jax.vjp(project, qkv_rows, gain_query, gain_key)
    query_low = head_outs[0].astype(BF16).reshape(row_count, HQ * HD)
    kv_low = jnp.concatenate([head_outs[1].astype(BF16), head_outs[2].astype(BF16)], axis=1)
    blocks = gather_blocks(kv_low.reshape(streams, SEG, 2 * HD))
    attn_low, lse = attention_forward(info, query_low, blocks)
    attn_proj = jnp.dot(attn_low, full_out, preferred_element_type=F32)
    post_attn, pull_attn = jax.vjp(rms_norm, attn_proj, gain_pa)
    middle = tok_rows + post_attn
    normed_ff, pull_ff = jax.vjp(rms_norm, middle, gain_pf)
    ff_low = normed_ff.astype(BF16)
    gate_up = jnp.dot(ff_low, full_gu, preferred_element_type=F32)
    hidden, pull_geglu = jax.vjp(geglu, gate_up)
    hidden_low = hidden.astype(BF16)
    down_proj = jnp.dot(hidden_low, full_down, preferred_element_type=F32)
    post_ff, pull_post = jax.vjp(rms_norm, down_proj, gain_po)
    layer_out = (middle + post_ff).astype(BF16).reshape(streams, SEG, D)
    grad_down, grad_gain_po = pull_post(grad_out)
    down_low = grad_down.astype(BF16)
    wgrad_down = jnp.dot(hidden_low.T, down_low, preferred_element_type=F32)
    grad_hidden = jnp.dot(down_low, full_down.T, preferred_element_type=F32)
    (grad_gate_up,) = pull_geglu(grad_hidden)
    gate_up_low = grad_gate_up.astype(BF16)
    wgrad_gu = jnp.dot(ff_low.T, gate_up_low, preferred_element_type=F32)
    grad_normed_ff = jnp.dot(gate_up_low, full_gu.T, preferred_element_type=F32)
    grad_middle_ff, grad_gain_pf = pull_ff(grad_normed_ff)
    grad_middle = grad_out + grad_middle_ff
    grad_attn_proj, grad_gain_pa = pull_attn(grad_middle)
    proj_low = grad_attn_proj.astype(BF16)
    wgrad_out = jnp.dot(attn_low.T, proj_low, preferred_element_type=F32)
    grad_attn_low = jnp.dot(proj_low, full_out.T, preferred_element_type=F32).astype(BF16)
    shard_gu = lax.psum_scatter(wgrad_gu.astype(BF16), "group", scatter_dimension=0, tiled=True)
    shard_mixed = lax.psum_scatter(
        jnp.concatenate(
            [
                wgrad_out.astype(BF16).reshape(MEMBERS, out_rows, D),
                wgrad_down.astype(BF16).reshape(MEMBERS, FF // MEMBERS, D),
            ],
            axis=1,
        ),
        "group",
        scatter_dimension=0,
        tiled=False,
    )
    grad_query, far, near_far, near = attention_backward(
        info, query_low, attn_low, grad_attn_low, lse, blocks
    )
    grad_kv = scatter_blocks(far, near_far, near).reshape(row_count, 2 * HD)
    grad_qkv, grad_gain_q, grad_gain_k = pull_heads(
        (grad_query.reshape(row_count, HQ, HD), grad_kv[:, :HD], grad_kv[:, HD:])
    )
    qkv_low = grad_qkv.astype(BF16)
    wgrad_qkv = jnp.dot(input_low.T, qkv_low, preferred_element_type=F32)
    grad_normed_in = jnp.dot(qkv_low, full_qkv.T, preferred_element_type=F32)
    grad_tokens_in, grad_gain_in = pull_in(grad_normed_in)
    token_grad = (grad_middle + grad_tokens_in).reshape(streams, SEG, D)
    wgrad_gains = jnp.concatenate(
        [grad_gain_in, grad_gain_pa, grad_gain_pf, grad_gain_po, grad_gain_q, grad_gain_k]
    )
    gains_out = jnp.pad(
        wgrad_gains.astype(BF16).reshape(MEMBERS, 1, gain_count),
        ((0, 0), (0, 0), (0, wgrad_qkv.shape[1] - gain_count)),
    )
    shard_first = lax.psum_scatter(
        jnp.concatenate(
            [wgrad_qkv.astype(BF16).reshape(MEMBERS, D // MEMBERS, -1), gains_out], axis=1
        ),
        "group",
        scatter_dimension=0,
        tiled=False,
    )

    def over_replicas(shard):
        if lax.axis_size("replica") == 2:
            other = lax.ppermute(shard, "replica", [(0, 1), (1, 0)])
            return shard.astype(F32) + other.astype(F32)
        return lax.psum(shard, "replica").astype(F32)

    sum_gu, sum_mixed, sum_first = (
        over_replicas(shard_gu),
        over_replicas(shard_mixed),
        over_replicas(shard_first),
    )
    shard_qkv, shard_gains = sum_first[:-1], sum_first[-1, :gain_count]
    shard_out, shard_down = sum_mixed[:out_rows], sum_mixed[out_rows:]
    upd_qkv = adam_step(w_qkv, first_qkv, second_qkv, shard_qkv, RATE_MATRIX, DECAY_RATE)
    upd_out = adam_step(w_out, first_out, second_out, shard_out, RATE_MATRIX, DECAY_RATE)
    upd_gu = adam_step(w_gu, first_gu, second_gu, sum_gu, RATE_MATRIX, DECAY_RATE)
    upd_down = adam_step(w_down, first_down, second_down, shard_down, RATE_MATRIX, DECAY_RATE)
    upd_gains = adam_step(norm_gains, first_gains, second_gains, shard_gains, RATE_GAIN, 0.0)
    return (layer_out, token_grad, *upd_qkv, *upd_out, *upd_gu, *upd_down, *upd_gains)


def solution(mesh):
    in_specs = (
        P("replica", "group", None),
        P("replica", "group", None),
        P("replica", None),
        P("group", None),
        P("group", None),
        P("group", None),
        P("group", None),
        P("group"),
        P("group", None),
        P("group", None),
        P("group", None),
        P("group", None),
        P("group"),
        P("group", None),
        P("group", None),
        P("group", None),
        P("group", None),
        P("group"),
    )
    out_specs = (
        P("replica", "group", None),
        P("replica", "group", None),
        P("group", None),
        P("group", None),
        P("group", None),
        P("group", None),
        P("group", None),
        P("group", None),
        P("group", None),
        P("group", None),
        P("group", None),
        P("group", None),
        P("group", None),
        P("group", None),
        P("group"),
        P("group"),
        P("group"),
    )
    return jax.shard_map(
        per_device, mesh=mesh, in_specs=in_specs, out_specs=out_specs, check_vma=False
    )
```

time: 871 us -> 505 us (0.58)
  waiting for transfers between devices: 499 us -> 297 us
  matrix products: 149 us -> 36.5 us
  blocking collectives: 71.5 us -> 0 us
  other arithmetic: 108 us -> 57.2 us
  Pallas kernels: 0 us -> 34.5 us
  starting transfers between devices: 1.12 us -> 26.8 us
  local copies, waits for them, and re-layouts: 21.7 us -> 31.3 us
    reduce_scatter x6 -> x3, waiting for transfers between devices: 319 us -> 128 us  [the longest x1 74.9 us: per_device(): lax.psum_scatter(wgrad_gu.astype(BF16), 'group', scatter_dimension=0, til...]
    ppermute x0 -> x29, waiting for transfers between devices: none -> 120 us  [the longest x6 93.6 us: step_z(): lax.ppermute(values, 'group', [(i, (i + 4) % MEMBERS) for i in range(MEMB...]
    dot_general x18 -> x12, matrix products: 149 us -> 36.5 us  [the longest x1 8.89 us: per_device(): wgrad_gu = jnp.dot(ff_low.T, gate_up_low, preferred_element_type=F32)]
    all_gather x6 -> x3, waiting for transfers between devices: 147 us -> 49.3 us  [the longest x1 42.1 us: per_device(): lax.all_gather(jnp.concatenate([qkv_rows_low, gain_row[None]], axis=0), '...]
    unnamed x2 -> x0, blocking collectives: 66.6 us -> none
    sub x2 -> x0, other arithmetic: 36.1 us -> none  [the longest x1 35.4 us: per_device(): exp_fwd = jnp.exp(score_fwd - row_max)]
    pallas_call x0 -> x2, Pallas kernels: none -> 34.5 us  [the longest x1 19.9 us: attention_backward(): pl.pallas_call(backward_kernel, out_shape=[jax.ShapeDtypeStruct((2 * SEG,...]
    psum x1 -> x0, waiting for transfers between devices: 32.5 us -> none  [per_device(): lax.psum(shard_qkv.astype(jnp.bfloat16), 'replica').astype(jnp.float32)]
  transfers between devices with their start and end apart: 13 -> 35, of which waited for: 13 -> 16; matrix products, arithmetic and copies ran while one was open for 19% -> 17% of each run, Pallas kernels for 0% -> 3%
where the time goes in v1:
time: 505 us; the launch traced here: 499 us
  waiting for transfers between devices  297 us (59%)
  other arithmetic  57.2 us (11%)
  matrix products  36.5 us (7%)
  Pallas kernels  34.5 us (7%)
  local copies, waits for them, and re-layouts  31.3 us (6%)
  starting transfers between devices  26.8 us (5%)
  between operations  15.6 us (3%)
    ppermute x6, waiting for transfers between devices, step_z(): lax.ppermute(values, 'group', [(i, (i + 4) % MEMBERS) for i in range(MEMB...  93.6 us
    reduce_scatter x1, waiting for transfers between devices, per_device(): lax.psum_scatter(wgrad_gu.astype(BF16), 'group', scatter_dimension=0, til...  74.9 us
    reduce_scatter x1, waiting for transfers between devices, per_device(): lax.psum_scatter(jnp.concatenate([wgrad_qkv.astype(BF16).reshape(MEMBERS,...  52.6 us
    all_gather x1, waiting for transfers between devices, per_device(): lax.all_gather(jnp.concatenate([qkv_rows_low, gain_row[None]], axis=0), '...  42.1 us
    pallas_call x1, Pallas kernels, attention_backward(): pl.pallas_call(backward_kernel, out_shape=[jax.ShapeDtypeStruct((2 * SEG,...  19.9 us
    pallas_call x1, Pallas kernels, attention_forward(): pl.pallas_call(forward_kernel, out_shape=(jax.ShapeDtypeStruct((2 * SEG,...  14.5 us
    ppermute x8, waiting for transfers between devices, swap_x(): return lax.ppermute(values, 'group', [(i, i ^ 2) for i in range(MEMBERS)])  14 us
    unnamed x182, local copies, waits for them, and re-layouts  13.3 us
  transfers between devices with their start and end apart: 35, of which 16 were waited for; matrix products, arithmetic and copies ran while one was open for 17% of the time, Pallas kernels for 3%

profile of v1, /device:TPU:0, one launch (start us, length us, event | category | flops | bytes accessed | tf_op | source)
XLA Modules:
  0.0 498.6 jit_solution(8417603068189072273)
XLA Ops:
  13.8 42.1 %all-gather.11.cloned.1.call-done = bf16[16,41,1536]{2,1,0:T(8,128)(2,1)} async-done(((bf16[1,41,1536]{2,1,0:T(8,128)(2,1)}), bf16[16,41,1536]{2,1,0:T(8,128)(2,1)}) %all-gather.11.cloned.1.call-update) | async-done | bytes 2015248 | tf_op jit(solution)/shard_map/all_gather | solution.py:394
  56.9 1.7 slice.138
  58.9 1.4 fusion.87
  60.6 1.9 fusion.58
  63.6 22.9 %collective-permute-done.1.refs_2_ = bf16[2,256,512]{2,1,0:T(8,128)(2,1)S(1)} collective-permute-done((bf16[2,256,512]{2,1,0:T(8,128)(2,1)S(1)}, bf16[2,256,512]{2,1,0:T(8,128)(2,1)S(1)}, u32[]{:S(2)}, u32[]{:S(2)}) %collective-permute-start.1) | collective-permute-done | bytes 524320 | tf_op jit(solution)/shard_map/ppermute | solution.py:110
  87.0 24.0 %collective-permute-done.3.refs_4_ = bf16[2,256,512]{2,1,0:T(8,128)(2,1)S(1)} collective-permute-done((bf16[2,256,512]{2,1,0:T(8,128)(2,1)S(1)}, bf16[2,256,512]{2,1,0:T(8,128)(2,1)S(1)}, u32[]{:S(2)}, u32[]{:S(2)}) %collective-permute-start.3) | collective-permute-done | bytes 524320 | tf_op jit(solution)/shard_map/ppermute | solution.py:110
  112.4 2.0 collective-permute-start.4
  114.4 14.0 %collective-permute-done.5.refs_6_ = bf16[2,256,512]{2,1,0:T(8,128)(2,1)} collective-permute-done((bf16[2,256,512]{2,1,0:T(8,128)(2,1)S(1)}, bf16[2,256,512]{2,1,0:T(8,128)(2,1)}, u32[]{:S(2)}, u32[]{:S(2)}) %collective-permute-start.5) | collective-permute-done | bytes 524320 | tf_op jit(solution)/shard_map/ppermute | solution.py:110
  128.4 3.2 slice.139
  131.6 3.2 reshape.317
  134.8 2.3 multiply_reduce_fusion.2
  138.5 8.7 %collective-permute-done.6.refs_7_ = bf16[2,256,512]{2,1,0:T(8,128)(2,1)} collective-permute-done((bf16[2,256,512]{2,1,0:T(8,128)(2,1)}, bf16[2,256,512]{2,1,0:T(8,128)(2,1)}, u32[]{:S(2)}, u32[]{:S(2)}) %collective-permute-start.6) | collective-permute-done | bytes 524320 | tf_op jit(solution)/shard_map/ppermute | solution.py:114
  147.2 2.0 multiply_multiply_fusion.3
  151.2 14.5 %attention_forward.1 = (bf16[512,1024]{1,0:T(8,128)(2,1)S(1)}, f32[2,1,1024]{2,1,0:T(1,128)S(1)}) custom-call(s32[6]{0:T(128)S(1)} %concatenate.29.info, bf16[512,1024]{1,0:T(8,128)(2,1)S(1)} %bitcast.139, bf16[2,256,512]{2,1,0:T(8,128)(2,1)S(1)} %bitcast.144, bf16[2,256,512]{2,1,0:T(8,128)(2,1)S(1)} %collective-permute-done.refs_1_, ...), custom_call_target="tpu_custom_call" | custom-call | flops 7000000000 | bytes 11000000 | tf_op jit(solution)/shard_map/attention_forward/pallas_call | solution.py:218
  170.8 1.4 slice.148
  172.3 4.1 slice.153
  177.9 7.1 %all-gather.7.cloned.1.call-done = bf16[640,4096]{1,0:T(8,128)(2,1)} async-done(((bf16[40,4096]{1,0:T(8,128)(2,1)}), bf16[640,4096]{1,0:T(8,128)(2,1)}) %all-gather.7.cloned.1.call-update) | async-done | bytes 5242896 | tf_op jit(solution)/shard_map/all_gather | solution.py:408
  185.1 5.5 %fusion.78 = f32[512,4096]{1,0:T(8,128)S(1)} fusion(bf16[640,4096]{1,0:T(8,128)(2,1)} %all-gather.7.cloned.1.call-done, f32[512,640]{1,0:T(8,128)S(1)} %get-tuple-element.76, f32[640]{0:T(1024)S(1)} %get-tuple-element.92, f32[512]{0:T(512)S(1)} %fusion.71), kind=kOutput, calls=%fused_computation.181 | convolution fusion | flops 2685337600 | bytes 14946816 | tf_op jit(solution)/shard_map/dot_general | solution.py:440
  190.6 1.5 multiply_convert_fusion
  192.3 1.9 multiply_reduce_fusion.7
  194.8 1.4 fusion.12
  196.2 4.9 fusion.10
  201.2 3.6 multiply_reduce_fusion.3
  206.0 1.5 copy-done.55
  207.5 2.0 convolution_convert_fusion.4.do_ref
  209.5 19.9 %attention_backward.1 = (f32[512,1024]{1,0:T(8,128)}, bf16[2,2,256,512]{3,2,1,0:T(8,128)(2,1)}, bf16[2,2,256,512]{3,2,1,0:T(8,128)(2,1)}, bf16[2,2,256,512]{3,2,...) custom-call(s32[6]{0:T(128)S(1)} %concatenate.29.info, ...), custom_call_target="tpu_custom_call" | custom-call | flops 16999999488 | bytes 24000000 | tf_op jit(solution)/shard_map/attention_backward/pallas_call | solution.py:341
  230.0 3.4 convolution_convert_fusion.1
  237.1 2.3 pad_maximum_fusion
  240.0 3.2 reshape.323
  243.2 1.6 convert_element_type.240
  245.1 1.5 collective-permute-start.20
  246.7 3.8 collective-permute-done.22
  250.5 1.3 fusion.28
  251.8 3.8 collective-permute-start.23
  258.0 2.1 collective-permute-start.18
  260.1 1.5 collective-permute-done.20
  261.6 6.5 %collective-permute-done.23 = bf16[2,256,512]{2,1,0:T(8,128)(2,1)S(1)} collective-permute-done((bf16[2,256,512]{2,1,0:T(8,128)(2,1)S(1)}, bf16[2,256,512]{2,1,0:T(8,128)(2,1)S(1)}, u32[]{:S(2)}, u32[]{:S(2)}) %collective-permute-start.23) | collective-permute-done | bytes 524320 | tf_op jit(solution)/shard_map/ppermute | solution.py:110
  269.2 3.6 collective-permute-start.24
  272.8 2.1 multiply_reduce_fusion
  275.1 1.7 convert_element_type.230
  278.8 12.7 %collective-permute-done.24 = bf16[2,256,512]{2,1,0:T(8,128)(2,1)} collective-permute-done((bf16[2,256,512]{2,1,0:T(8,128)(2,1)}, bf16[2,256,512]{2,1,0:T(8,128)(2,1)}, u32[]{:S(2)}, u32[]{:S(2)}) %collective-permute-start.24) | collective-permute-done | bytes 524320 | tf_op jit(solution)/shard_map/ppermute | solution.py:110
  291.4 2.3 fusion.40
  293.8 1.4 collective-permute-start.25
  295.3 3.3 add_add_fusion
  299.2 13.6 %collective-permute-done.25 = bf16[2,256,512]{2,1,0:T(8,128)(2,1)} collective-permute-done((bf16[2,256,512]{2,1,0:T(8,128)(2,1)}, bf16[2,256,512]{2,1,0:T(8,128)(2,1)}, u32[]{:S(2)}, u32[]{:S(2)}) %collective-permute-start.25) | collective-permute-done | bytes 524320 | tf_op jit(solution)/shard_map/ppermute | solution.py:110
  312.8 1.3 fusion.45
  315.4 1.3 multiply_reduce_fusion.10
  316.7 1.2 add_add_fusion.5
  318.0 1.6 fusion.19
  321.0 1.5 fusion.18
  323.3 1.2 convolution_convert_fusion.2
  324.5 1.6 fusion.7
  326.2 1.2 copy-done.21
  327.4 8.9 %convolution_convert_fusion = bf16[640,4096]{1,0:T(8,128)(2,1)} fusion(f32[512,2048]{1,0:T(8,128)} %copy-done.39, f32[512,2048]{1,0:T(8,128)} %copy-done.38, f32[512,640]{1,0:T(8,128)S(1)} %copy-done.21, f32[640]{0:T(1024)S(1)} %get-tuple-element.92, f32[512]{0:T(512)S(1)} %fusion.71), kind=kOutput, calls=%fused_computation.1 | convolution fusion | flops 2692153344 | bytes 14946816 | tf_op jit(solution)/shard_map/dot_general | solution.py:452
  336.4 3.7 collective-permute-start.27
  340.1 4.4 collective-permute-done.27
  346.6 52.6 %reduce-scatter.4.cloned.1.call-done = bf16[1,41,1536]{2,1,0:T(8,128)(2,1)} async-done(((bf16[16,41,1536]{2,1,0:T(8,128)(2,1)}), bf16[1,41,1536]{2,1,0:T(8,128)(2,1)}) %reduce-scatter.4.cloned.1.call-update) | async-done | bytes 125968 | tf_op jit(solution)/shard_map/reduce_scatter | solution.py:492
  399.2 1.4 collective-permute-start.26
  400.6 1.7 divide_subtract_fusion.3
  402.3 2.2 collective-permute-done.26
  405.5 74.9 %reduce-scatter.8.cloned.1.call-done = bf16[40,4096]{1,0:T(8,128)(2,1)} async-done(((bf16[640,4096]{1,0:T(8,128)(2,1)}), bf16[40,4096]{1,0:T(8,128)(2,1)}) %reduce-scatter.8.cloned.1.call-update) | async-done | bytes 327696 | tf_op jit(solution)/shard_map/reduce_scatter | solution.py:460
  480.4 1.4 collective-permute-start.28
  483.4 5.6 %collective-permute-done.28 = bf16[40,4096]{1,0:T(8,128)(2,1)S(1)} collective-permute-done((bf16[40,4096]{1,0:T(8,128)(2,1)}, bf16[40,4096]{1,0:T(8,128)(2,1)S(1)}, u32[]{:S(2)}, u32[]{:S(2)}) %collective-permute-start.28) | collective-permute-done | bytes 327712 | tf_op jit(solution)/shard_map/ppermute | solution.py:503
  489.0 2.5 divide_subtract_fusion
  (300 shorter events, 42.2 us)
Async XLA Ops:
  7.2 48.7 %all-gather.11.cloned.1.call-start = ((), (), s32[]{:S(2)}) async-start(), calls=%async_computation.8 | async-start | bytes 2506752 | tf_op jit(solution)/shard_map/all_gather | solution.py:394
  9.7 161.1 %all-gather.9.cloned.1.call-start = ((), (), s32[]{:S(2)}) async-start(), calls=%async_computation.7 | async-start | bytes 4177920 | tf_op jit(solution)/shard_map/all_gather | solution.py:400
  12.4 172.6 %all-gather.7.cloned.1.call-start = ((), (), s32[]{:S(2)}) async-start(), calls=%async_computation.3 | async-start | bytes 5570560 | tf_op jit(solution)/shard_map/all_gather | solution.py:408
  13.3 323.1 %reduce-scatter.6.cloned.1.call-start = ((), (), s32[]{:S(2)}) async-start(), calls=%async_computation.5 | async-start | bytes 4177920 | tf_op jit(solution)/shard_map/reduce_scatter | solution.py:461
  62.6 88.1 %copy-start.1 = (bf16[512,512]{1,0:T(8,128)(2,1)}, bf16[512,512]{1,0:T(8,128)(2,1)S(1)}, u32[]{:S(2)}) copy-start(bf16[512,512]{1,0:T(8,128)(2,1)S(1)} %pad_maximum_fusion.2) | copy-start | bytes 1572868
  62.6 23.9 %collective-permute-start.1 = (bf16[2,256,512]{2,1,0:T(8,128)(2,1)S(1)}, bf16[2,256,512]{2,1,0:T(8,128)(2,1)S(1)}, u32[]{:S(2)}, u32[]{:S(2)}) collective-permute-start(bf16[2,256,512]{2,1,0:T(8,128)(2,1)S(1)} %bitcast.141), channel_id=1, source_target_pairs={{0,4},{1,5},{2,6},{3,7},{4,8},{5,9},{6,10},{7,11},{8,12},{9,13},{1... | collective-permute-start | bytes 1572872 | tf_op jit(solution)/shard_map/ppermute | solution.py:110
  86.5 64.2 %copy-start.2 = (bf16[2,256,512]{2,1,0:T(8,128)(2,1)}, bf16[2,256,512]{2,1,0:T(8,128)(2,1)S(1)}, u32[]{:S(2)}) copy-start(bf16[2,256,512]{2,1,0:T(8,128)(2,1)S(1)} %collective-permute-done.1.refs_2_) | copy-start | bytes 1572868
  86.5 24.5 %collective-permute-start.3 = (bf16[2,256,512]{2,1,0:T(8,128)(2,1)S(1)}, bf16[2,256,512]{2,1,0:T(8,128)(2,1)S(1)}, u32[]{:S(2)}, u32[]{:S(2)}) collective-permute-start(bf16[2,256,512]{2,1,0:T(8,128)(2,1)S(1)} %collective-permute-done.1.refs_2_), channel_id=1, source_target_pairs={{0,4},{1,5},{2,6},{3,7},{4,8},{5,9},{6,10},{7,11},{8,12},{9,13},{1... | collective-permute-start | bytes 1572872 | tf_op jit(solution)/shard_map/ppermute | solution.py:110
  86.5 24.6 %collective-permute-start = (bf16[2,256,512]{2,1,0:T(8,128)(2,1)S(1)}, bf16[2,256,512]{2,1,0:T(8,128)(2,1)S(1)}, u32[]{:S(2)}, u32[]{:S(2)}) collective-permute-start(bf16[2,256,512]{2,1,0:T(8,128)(2,1)S(1)} %bitcast.142), channel_id=1, source_target_pairs={{0,2},{1,3},{2,0},{3,1},{4,6},{5,7},{6,4},{7,5},{8,10},{9,11},{10,... | collective-permute-start | bytes 1572872 | tf_op jit(solution)/shard_map/ppermute | solution.py:114
  87.0 24.6 %collective-permute-start.7 = (bf16[2,256,512]{2,1,0:T(8,128)(2,1)S(1)}, bf16[2,256,512]{2,1,0:T(8,128)(2,1)S(1)}, u32[]{:S(2)}, u32[]{:S(2)}) collective-permute-start(bf16[2,256,512]{2,1,0:T(8,128)(2,1)S(1)} %bitcast.143), channel_id=1, source_target_pairs={{0,1},{1,0},{2,3},{3,2},{4,5},{5,4},{6,7},{7,6},{8,9},{9,8},{10,11... | collective-permute-start | bytes 1572872 | tf_op jit(solution)/shard_map/ppermute | solution.py:118
  111.0 39.7 %copy-start.3 = (bf16[2,256,512]{2,1,0:T(8,128)(2,1)}, bf16[2,256,512]{2,1,0:T(8,128)(2,1)S(1)}, u32[]{:S(2)}) copy-start(bf16[2,256,512]{2,1,0:T(8,128)(2,1)S(1)} %collective-permute-done.3.refs_4_) | copy-start | bytes 1572868
  111.0 17.3 %collective-permute-start.5 = (bf16[2,256,512]{2,1,0:T(8,128)(2,1)S(1)}, bf16[2,256,512]{2,1,0:T(8,128)(2,1)}, u32[]{:S(2)}, u32[]{:S(2)}) collective-permute-start(bf16[2,256,512]{2,1,0:T(8,128)(2,1)S(1)} %collective-permute-done.3.refs_4_), channel_id=1, source_target_pairs={{0,4},{1,5},{2,6},{3,7},{4,8},{5,9},{6,10},{7,11},{8,12},{9,13},{1... | collective-permute-start | bytes 1572872 | tf_op jit(solution)/shard_map/ppermute | solution.py:110
  111.0 26.4 %collective-permute-start.2 = (bf16[2,256,512]{2,1,0:T(8,128)(2,1)S(1)}, bf16[2,256,512]{2,1,0:T(8,128)(2,1)}, u32[]{:S(2)}, u32[]{:S(2)}) collective-permute-start(bf16[2,256,512]{2,1,0:T(8,128)(2,1)S(1)} %collective-permute-done.1.refs_2_), channel_id=1, source_target_pairs={{0,2},{1,3},{2,0},{3,1},{4,6},{5,7},{6,4},{7,5},{8,10},{9,11},{10,... | collective-permute-start | bytes 1572872 | tf_op jit(solution)/shard_map/ppermute | solution.py:114
  111.0 26.5 %collective-permute-start.9 = (bf16[2,256,512]{2,1,0:T(8,128)(2,1)S(1)}, bf16[2,256,512]{2,1,0:T(8,128)(2,1)S(1)}, u32[]{:S(2)}, u32[]{:S(2)}) collective-permute-start(bf16[2,256,512]{2,1,0:T(8,128)(2,1)S(1)} %collective-permute-done.1.refs_2_), channel_id=1, source_target_pairs={{0,1},{1,0},{2,3},{3,2},{4,5},{5,4},{6,7},{7,6},{8,9},{9,8},{10,11... | collective-permute-start | bytes 1572872 | tf_op jit(solution)/shard_map/ppermute | solution.py:118
  111.1 39.6 %copy-start.4 = (bf16[2,256,512]{2,1,0:T(8,128)(2,1)}, bf16[2,256,512]{2,1,0:T(8,128)(2,1)S(1)}, u32[]{:S(2)}) copy-start(bf16[2,256,512]{2,1,0:T(8,128)(2,1)S(1)} %collective-permute-done.refs_1_) | copy-start | bytes 1572868
  111.1 26.9 %collective-permute-start.8 = (bf16[2,256,512]{2,1,0:T(8,128)(2,1)S(1)}, bf16[2,256,512]{2,1,0:T(8,128)(2,1)S(1)}, u32[]{:S(2)}, u32[]{:S(2)}) collective-permute-start(bf16[2,256,512]{2,1,0:T(8,128)(2,1)S(1)} %collective-permute-done.refs_1_), channel_id=1, source_target_pairs={{0,1},{1,0},{2,3},{3,2},{4,5},{5,4},{6,7},{7,6},{8,9},{9,8},{10,11... | collective-permute-start | bytes 1572872 | tf_op jit(solution)/shard_map/ppermute | solution.py:118
  112.4 25.7 %collective-permute-start.4 = (bf16[2,256,512]{2,1,0:T(8,128)(2,1)S(1)}, bf16[2,256,512]{2,1,0:T(8,128)(2,1)}, u32[]{:S(2)}, u32[]{:S(2)}) collective-permute-start(bf16[2,256,512]{2,1,0:T(8,128)(2,1)S(1)} %collective-permute-done.3.refs_4_), channel_id=1, source_target_pairs={{0,2},{1,3},{2,0},{3,1},{4,6},{5,7},{6,4},{7,5},{8,10},{9,11},{10,... | collective-permute-start | bytes 1572872 | tf_op jit(solution)/shard_map/ppermute | solution.py:114
  128.3 18.8 %collective-permute-start.6 = (bf16[2,256,512]{2,1,0:T(8,128)(2,1)}, bf16[2,256,512]{2,1,0:T(8,128)(2,1)}, u32[]{:S(2)}, u32[]{:S(2)}) collective-permute-start(bf16[2,256,512]{2,1,0:T(8,128)(2,1)} %collective-permute-done.5.refs_6_), channel_id=1, source_target_pairs={{0,2},{1,3},{2,0},{3,1},{4,6},{5,7},{6,4},{7,5},{8,10},{9,11},{10,... | collective-permute-start | bytes 1572872 | tf_op jit(solution)/shard_map/ppermute | solution.py:114
  137.4 13.3 %collective-permute-start.11 = (bf16[2,256,512]{2,1,0:T(8,128)(2,1)S(1)}, bf16[2,256,512]{2,1,0:T(8,128)(2,1)S(1)}, u32[]{:S(2)}, u32[]{:S(2)}) collective-permute-start(bf16[2,256,512]{2,1,0:T(8,128)(2,1)S(1)} %collective-permute-done.3.refs_4_), channel_id=1, source_target_pairs={{0,1},{1,0},{2,3},{3,2},{4,5},{5,4},{6,7},{7,6},{8,9},{9,8},{10,11... | collective-permute-start | bytes 1572872 | tf_op jit(solution)/shard_map/ppermute | solution.py:118
  137.5 13.2 %collective-permute-start.10 = (bf16[2,256,512]{2,1,0:T(8,128)(2,1)}, bf16[2,256,512]{2,1,0:T(8,128)(2,1)S(1)}, u32[]{:S(2)}, u32[]{:S(2)}) collective-permute-start(bf16[2,256,512]{2,1,0:T(8,128)(2,1)} %collective-permute-done.2.refs_3_), channel_id=1, source_target_pairs={{0,1},{1,0},{2,3},{3,2},{4,5},{5,4},{6,7},{7,6},{8,9},{9,8},{10,11... | collective-permute-start | bytes 1572872 | tf_op jit(solution)/shard_map/ppermute | solution.py:118
  138.0 12.7 %collective-permute-start.13 = (bf16[2,256,512]{2,1,0:T(8,128)(2,1)}, bf16[2,256,512]{2,1,0:T(8,128)(2,1)S(1)}, u32[]{:S(2)}, u32[]{:S(2)}) collective-permute-start(bf16[2,256,512]{2,1,0:T(8,128)(2,1)} %collective-permute-done.5.refs_6_), channel_id=1, source_target_pairs={{0,1},{1,0},{2,3},{3,2},{4,5},{5,4},{6,7},{7,6},{8,9},{9,8},{10,11... | collective-permute-start | bytes 1572872 | tf_op jit(solution)/shard_map/ppermute | solution.py:118
  138.1 12.6 %collective-permute-start.12 = (bf16[2,256,512]{2,1,0:T(8,128)(2,1)}, bf16[2,256,512]{2,1,0:T(8,128)(2,1)S(1)}, u32[]{:S(2)}, u32[]{:S(2)}) collective-permute-start(bf16[2,256,512]{2,1,0:T(8,128)(2,1)} %collective-permute-done.4.refs_5_), channel_id=1, source_target_pairs={{0,1},{1,0},{2,3},{3,2},{4,5},{5,4},{6,7},{7,6},{8,9},{9,8},{10,11... | collective-permute-start | bytes 1572872 | tf_op jit(solution)/shard_map/ppermute | solution.py:118
  147.2 3.5 collective-permute-start.14
  150.6 15.1 %copy-start = (bf16[64,8,4,256]{3,1,2,0:T(8,128)(2,1)}, bf16[64,8,4,256]{3,1,2,0:T(8,128)(2,1)S(1)}, u32[]{:S(2)}) copy-start(bf16[64,8,4,256]{3,1,2,0:T(8,128)(2,1)S(1)} %copy.48) | copy-start | bytes 3145732
  177.9 26.9 %copy-start.20 = (f32[512,640]{1,0:T(8,128)}, f32[512,640]{1,0:T(8,128)S(1)}, u32[]{:S(2)}) copy-start(f32[512,640]{1,0:T(8,128)S(1)} %get-tuple-element.76) | copy-start | bytes 3932164
  209.5 20.5 %copy-start.61 = (bf16[512,640]{1,0:T(8,128)(2,1)S(1)}, bf16[512,640]{1,0:T(8,128)(2,1)}, u32[]{:S(2)}) copy-start(bf16[512,640]{1,0:T(8,128)(2,1)} %copy-done.60) | copy-start | bytes 1966084
  229.4 4.1 collective-permute-start.21
  229.7 13.5 %collective-permute-start.19 = (bf16[2,2,256,512]{3,2,1,0:T(8,128)(2,1)}, bf16[2,2,256,512]{3,2,1,0:T(8,128)(2,1)}, u32[]{:S(2)}, u32[]{:S(2)}) collective-permute-start(bf16[2,2,256,512]{3,2,1,0:T(8,128)(2,1)} %get-tuple-element.41), channel_id=1, source_target_pairs={{0,1},{1,0},{2,3},{3,2},{4,5},{5,4},{6,7},{7,6},{8,9},{9,8},{10,11... | collective-permute-start | bytes 3145736 | tf_op jit(solution)/shard_map/ppermute | solution.py:118
  235.4 15.1 %collective-permute-start.22 = (bf16[2,256,512]{2,1,0:T(8,128)(2,1)}, bf16[2,256,512]{2,1,0:T(8,128)(2,1)}, u32[]{:S(2)}, u32[]{:S(2)}) collective-permute-start(bf16[2,256,512]{2,1,0:T(8,128)(2,1)} %fusion.25), channel_id=1, source_target_pairs={{0,2},{1,3},{2,0},{3,1},{4,6},{5,7},{6,4},{7,5},{8,10},{9,11},{10,... | collective-permute-start | bytes 1572872 | tf_op jit(solution)/shard_map/ppermute | solution.py:114
  237.0 19.2 %collective-permute-start.17 = (bf16[2,2,256,512]{3,2,1,0:T(8,128)(2,1)}, bf16[2,2,256,512]{3,2,1,0:T(8,128)(2,1)S(1)}, u32[]{:S(2)}, u32[]{:S(2)}) collective-permute-start(bf16[2,2,256,512]{3,2,1,0:T(8,128)(2,1)} %get-tuple-element.38), channel_id=1, source_target_pairs={{0,1},{1,0},{2,3},{3,2},{4,5},{5,4},{6,7},{7,6},{8,9},{9,8},{10,11... | collective-permute-start | bytes 3145736 | tf_op jit(solution)/shard_map/ppermute | solution.py:118
  239.4 159.8 %reduce-scatter.4.cloned.1.call-start = ((), (), s32[]{:S(2)}) async-start(), calls=%async_computation.4 | async-start | bytes 2506752 | tf_op jit(solution)/shard_map/reduce_scatter | solution.py:492
  239.5 35.6 %collective-permute-start.15 = (bf16[2,2,256,512]{3,2,1,0:T(8,128)(2,1)}, bf16[2,2,256,512]{3,2,1,0:T(8,128)(2,1)}, u32[]{:S(2)}, u32[]{:S(2)}) collective-permute-start(bf16[2,2,256,512]{3,2,1,0:T(8,128)(2,1)} %get-tuple-element.35), channel_id=1, source_target_pairs={{0,1},{1,0},{2,3},{3,2},{4,5},{5,4},{6,7},{7,6},{8,9},{9,8},{10,11... | collective-permute-start | bytes 3145736 | tf_op jit(solution)/shard_map/ppermute | solution.py:118
  245.1 16.5 %collective-permute-start.20 = (bf16[2,256,512]{2,1,0:T(8,128)(2,1)S(1)}, bf16[2,256,512]{2,1,0:T(8,128)(2,1)S(1)}, u32[]{:S(2)}, u32[]{:S(2)}) collective-permute-start(bf16[2,256,512]{2,1,0:T(8,128)(2,1)S(1)} %fusion.30), channel_id=1, source_target_pairs={{0,2},{1,3},{2,0},{3,1},{4,6},{5,7},{6,4},{7,5},{8,10},{9,11},{10,... | collective-permute-start | bytes 1572872 | tf_op jit(solution)/shard_map/ppermute | solution.py:114
  251.8 16.3 %collective-permute-start.23 = (bf16[2,256,512]{2,1,0:T(8,128)(2,1)S(1)}, bf16[2,256,512]{2,1,0:T(8,128)(2,1)S(1)}, u32[]{:S(2)}, u32[]{:S(2)}) collective-permute-start(bf16[2,256,512]{2,1,0:T(8,128)(2,1)S(1)} %fusion.28), channel_id=1, source_target_pairs={{0,4},{1,5},{2,6},{3,7},{4,8},{5,9},{6,10},{7,11},{8,12},{9,13},{1... | collective-permute-start | bytes 1572872 | tf_op jit(solution)/shard_map/ppermute | solution.py:110
  256.1 16.7 %copy-start.27 = (f32[512,4,128]{2,1,0:T(4,128)}, f32[512,4,128]{2,1,0:T(4,128)S(1)}, u32[]{:S(2)}) copy-start(f32[512,4,128]{2,1,0:T(4,128)S(1)} %get-tuple-element.79) | copy-start | bytes 3145732
  256.2 16.7 %copy-start.28 = (f32[512,4,128]{2,1,0:T(4,128)}, f32[512,4,128]{2,1,0:T(4,128)S(1)}, u32[]{:S(2)}) copy-start(f32[512,4,128]{2,1,0:T(4,128)S(1)} %get-tuple-element.80) | copy-start | bytes 3145732
  256.2 11.9 %copy-start.70 = (bf16[2,256,512]{2,1,0:T(8,128)(2,1)S(1)}, bf16[2,256,512]{2,1,0:T(8,128)(2,1)}, u32[]{:S(2)}) copy-start(bf16[2,256,512]{2,1,0:T(8,128)(2,1)} %get-tuple-element.40) | copy-start | bytes 1572868
  258.0 14.8 %copy-start.19 = (f32[512,4,256]{2,1,0:T(4,128)S(1)}, f32[512,4,256]{2,1,0:T(4,128)}, u32[]{:S(2)}) copy-start(f32[512,4,256]{2,1,0:T(4,128)} %reshape.317) | copy-start | bytes 6291460
  258.0 14.8 %copy-start.41 = (f32[512,4]{1,0:T(8,128)S(1)}, f32[512,4]{1,0:T(8,128)}, u32[]{:S(2)}) copy-start(f32[512,4]{1,0:T(8,128)} %copy-done.40) | copy-start | bytes 24580
  258.0 20.8 %collective-permute-start.18 = (bf16[2,256,512]{2,1,0:T(8,128)(2,1)}, bf16[2,256,512]{2,1,0:T(8,128)(2,1)}, u32[]{:S(2)}, u32[]{:S(2)}) collective-permute-start(bf16[2,256,512]{2,1,0:T(8,128)(2,1)} %fusion.36), channel_id=1, source_target_pairs={{0,2},{1,3},{2,0},{3,1},{4,6},{5,7},{6,4},{7,5},{8,10},{9,11},{10,... | collective-permute-start | bytes 1572872 | tf_op jit(solution)/shard_map/ppermute | solution.py:114
  269.2 22.2 %collective-permute-start.24 = (bf16[2,256,512]{2,1,0:T(8,128)(2,1)}, bf16[2,256,512]{2,1,0:T(8,128)(2,1)}, u32[]{:S(2)}, u32[]{:S(2)}) collective-permute-start(bf16[2,256,512]{2,1,0:T(8,128)(2,1)} %fusion.34), channel_id=1, source_target_pairs={{0,4},{1,5},{2,6},{3,7},{4,8},{5,9},{6,10},{7,11},{8,12},{9,13},{1... | collective-permute-start | bytes 1572872 | tf_op jit(solution)/shard_map/ppermute | solution.py:110
  275.1 16.4 %copy-start.30 = (f32[2,2,256,512]{3,2,1,0:T(8,128)S(1)}, f32[2,2,256,512]{3,2,1,0:T(8,128)}, u32[]{:S(2)}) copy-start(f32[2,2,256,512]{3,2,1,0:T(8,128)} %copy-done.29) | copy-start | bytes 6291460
  275.1 16.4 %copy-start.69 = (bf16[2,256,512]{2,1,0:T(8,128)(2,1)S(1)}, bf16[2,256,512]{2,1,0:T(8,128)(2,1)}, u32[]{:S(2)}) copy-start(bf16[2,256,512]{2,1,0:T(8,128)(2,1)} %get-tuple-element.37) | copy-start | bytes 1572868
  276.8 17.0 %copy-start.33 = (f32[2,2,256,512]{3,2,1,0:T(8,128)}, f32[2,2,256,512]{3,2,1,0:T(8,128)S(1)}, u32[]{:S(2)}) copy-start(f32[2,2,256,512]{3,2,1,0:T(8,128)S(1)} %convert_element_type.230) | copy-start | bytes 6291460
  278.0 21.2 %collective-permute-start.16 = (bf16[2,256,512]{2,1,0:T(8,128)(2,1)}, bf16[2,256,512]{2,1,0:T(8,128)(2,1)S(1)}, u32[]{:S(2)}, u32[]{:S(2)}) collective-permute-start(bf16[2,256,512]{2,1,0:T(8,128)(2,1)} %fusion.42), channel_id=1, source_target_pairs={{0,2},{1,3},{2,0},{3,1},{4,6},{5,7},{6,4},{7,5},{8,10},{9,11},{10,... | collective-permute-start | bytes 1572872 | tf_op jit(solution)/shard_map/ppermute | solution.py:114
  293.8 19.0 %collective-permute-start.25 = (bf16[2,256,512]{2,1,0:T(8,128)(2,1)}, bf16[2,256,512]{2,1,0:T(8,128)(2,1)}, u32[]{:S(2)}, u32[]{:S(2)}) collective-permute-start(bf16[2,256,512]{2,1,0:T(8,128)(2,1)} %fusion.40), channel_id=1, source_target_pairs={{0,4},{1,5},{2,6},{3,7},{4,8},{5,9},{6,10},{7,11},{8,12},{9,13},{1... | collective-permute-start | bytes 1572872 | tf_op jit(solution)/shard_map/ppermute | solution.py:110
  298.7 14.2 %copy-start.34 = (f32[2,2,256,512]{3,2,1,0:T(8,128)S(1)}, f32[2,2,256,512]{3,2,1,0:T(8,128)}, u32[]{:S(2)}) copy-start(f32[2,2,256,512]{3,2,1,0:T(8,128)} %copy-done.33) | copy-start | bytes 6291460
  298.7 14.1 %copy-start.65 = (bf16[2,256,512]{2,1,0:T(8,128)(2,1)S(1)}, bf16[2,256,512]{2,1,0:T(8,128)(2,1)}, u32[]{:S(2)}) copy-start(bf16[2,256,512]{2,1,0:T(8,128)(2,1)} %get-tuple-element.34) | copy-start | bytes 1572868
  299.1 18.9 %copy-start.50 = (f32[64,8,4,256]{3,1,2,0:T(8,128)}, f32[64,8,4,256]{3,1,2,0:T(8,128)S(1)}, u32[]{:S(2)}) copy-start(f32[64,8,4,256]{3,1,2,0:T(8,128)S(1)} %copy.49) | copy-start | bytes 6291460
  326.1 154.3 %reduce-scatter.8.cloned.1.call-start = ((), (), s32[]{:S(2)}) async-start(), calls=%async_computation.6 | async-start | bytes 5570560 | tf_op jit(solution)/shard_map/reduce_scatter | solution.py:460
  336.3 64.2 %copy-start.62 = (f32[64,640]{1,0:T(8,128)S(1)}, f32[64,640]{1,0:T(8,128)}, u32[]{:S(2)}) copy-start(f32[64,640]{1,0:T(8,128)} %param.22) | copy-start | bytes 491524
  336.4 64.2 %copy-start.78 = (f32[64,640]{1,0:T(8,128)S(1)}, f32[64,640]{1,0:T(8,128)}, u32[]{:S(2)}) copy-start(f32[64,640]{1,0:T(8,128)} %param.32) | copy-start | bytes 491524
  336.4 8.0 %collective-permute-start.27 = (bf16[192,640]{1,0:T(8,128)(2,1)}, bf16[192,640]{1,0:T(8,128)(2,1)S(1)}, u32[]{:S(2)}, u32[]{:S(2)}) collective-permute-start(bf16[192,640]{1,0:T(8,128)(2,1)} %bitcast.168), channel_id=1, source_target_pairs={{0,16},{16,0},{1,17},{17,1},{2,18},{18,2},{3,19},{19,3},{4,20},{20... | collective-permute-start | bytes 737288 | tf_op jit(solution)/shard_map/ppermute | solution.py:503
  345.5 136.3 %copy-start.57 = (f32[40,1536]{1,0:T(8,128)S(1)}, f32[40,1536]{1,0:T(8,128)}, u32[]{:S(2)}) copy-start(f32[40,1536]{1,0:T(8,128)} %param.21) | copy-start | bytes 737284
  345.5 136.3 %copy-start.76 = (f32[40,1536]{1,0:T(8,128)S(1)}, f32[40,1536]{1,0:T(8,128)}, u32[]{:S(2)}) copy-start(f32[40,1536]{1,0:T(8,128)} %param.31) | copy-start | bytes 737284
  345.5 136.3 %copy-start.77 = (f32[40,1536]{1,0:T(8,128)S(1)}, f32[40,1536]{1,0:T(8,128)}, u32[]{:S(2)}) copy-start(f32[40,1536]{1,0:T(8,128)} %param.26) | copy-start | bytes 737284
  346.6 136.2 %copy-start.79 = (f32[192]{0:T(256)S(1)}, f32[192]{0:T(256)}, u32[]{:S(2)}) copy-start(f32[192]{0:T(256)} %param.25) | copy-start | bytes 2308
  346.6 136.2 %copy-start.80 = (f32[192]{0:T(256)S(1)}, f32[192]{0:T(256)}, u32[]{:S(2)}) copy-start(f32[192]{0:T(256)} %param.35) | copy-start | bytes 2308
  346.6 136.2 %copy-start.81 = (f32[192]{0:T(256)S(1)}, f32[192]{0:T(256)}, u32[]{:S(2)}) copy-start(f32[192]{0:T(256)} %param.30) | copy-start | bytes 2308
  346.6 142.4 %copy-start.44 = (f32[40,4096]{1,0:T(8,128)S(1)}, f32[40,4096]{1,0:T(8,128)}, u32[]{:S(2)}) copy-start(f32[40,4096]{1,0:T(8,128)} %param.23) | copy-start | bytes 1966084
  346.6 142.4 %copy-start.58 = (f32[40,4096]{1,0:T(8,128)S(1)}, f32[40,4096]{1,0:T(8,128)}, u32[]{:S(2)}) copy-start(f32[40,4096]{1,0:T(8,128)} %param.33) | copy-start | bytes 1966084
  346.6 142.4 %copy-start.59 = (f32[40,4096]{1,0:T(8,128)S(1)}, f32[40,4096]{1,0:T(8,128)}, u32[]{:S(2)}) copy-start(f32[40,4096]{1,0:T(8,128)} %param.28) | copy-start | bytes 1966084
  399.2 5.4 %collective-permute-start.26 = (bf16[41,1536]{1,0:T(8,128)(2,1)}, bf16[41,1536]{1,0:T(8,128)(2,1)S(1)}, u32[]{:S(2)}, u32[]{:S(2)}) collective-permute-start(bf16[41,1536]{1,0:T(8,128)(2,1)} %bitcast.169), channel_id=1, source_target_pairs={{0,16},{16,0},{1,17},{17,1},{2,18},{18,2},{3,19},{19,3},{4,20},{20... | collective-permute-start | bytes 377864 | tf_op jit(solution)/shard_map/ppermute | solution.py:503
  480.4 8.5 %collective-permute-start.28 = (bf16[40,4096]{1,0:T(8,128)(2,1)}, bf16[40,4096]{1,0:T(8,128)(2,1)S(1)}, u32[]{:S(2)}, u32[]{:S(2)}) collective-permute-start(bf16[40,4096]{1,0:T(8,128)(2,1)} %reduce-scatter.8.cloned.1.call-done), channel_id=1, source_target_pairs={{0,16},{16,0},{1,17},{17,1},{2,18},{18,2},{3,19},{19,3},{4,20},{20... | collective-permute-start | bytes 983048 | tf_op jit(solution)/shard_map/ppermute | solution.py:503
  (56 other events, 226.5 us)
Sparse Core Ops, SparseCore 0:
  10.9 45.0 all-gather.10
  58.8 68.0 all-gather.8
  129.7 55.2 all-gather.6
  239.5 93.6 reduce-scatter.5
  337.3 61.8 reduce-scatter.3
  402.9 77.4 reduce-scatter.7
